TPU v7x, 512 devices: a whole 4x8x8 slice. The times are simulated.
512 devices in a mesh: gz: 64 (over z, y), gy: 8 (over x, core).
Axes of the slice: x: 4, y: 8, z: 8, core: 2. Of those that a mesh axis runs over, the one named last changes fastest.
Arguments:
- source: float32 [128, 512, 512], P('gz', 'gy'), may hold values from -6 to 6
- screening: float32 [128], replicated, may hold values from 1e-05 to 0.002
Outputs:
- pressure: float32 [128, 512, 512], P('gz', 'gy')
All inputs are finite; a program needn't handle non-finite values.
Results may differ from a plain program's by a relative error of at most 0.00045.
Values sent between devices are 32-bit elements; how exact they have to be, the bound alone decides.
No kernel may reach another device: no remote copies, remote signals or barrier semaphores. Data moves between devices by JAX's collectives and lax.ppermute only.
A program may use at most 192 MiB of HBM per device.

v0:
```python
import math

import jax
import jax.numpy as jnp
from jax import lax
from jax.sharding import PartitionSpec as P

NX = 512
NY = 512


def carried_in(value, axis, join, neutral, backward):
    count, mine = (lax.axis_size(axis), lax.axis_index(axis))
    pieces = jax.tree.map(lambda part: lax.all_gather(part, axis), value)
    if backward:
        pieces = jax.tree.map(lambda part: part[::-1], pieces)
        mine = count - 1 - mine
    so_far = jax.tree.map(
        lambda part, zero: jnp.full_like(part, 0) + jnp.asarray(zero, part.dtype), value, neutral
    )

    def lap(position, so_far):
        longer = join(so_far, jax.tree.map(lambda part: part[position], pieces))
        return jax.tree.map(lambda new, old: jnp.where(position < mine, new, old), longer, so_far)

    return lax.fori_loop(0, count - 1, lap, so_far)


def cas_table(count):
    index = jnp.arange(count, dtype=jnp.int32)
    phase = index[:, None] * index[None, :] % count
    angle = phase.astype(jnp.float32) * (2.0 * math.pi / count)
    return jnp.cos(angle) + jnp.sin(angle)


def wave_term(first, count, total):
    index = first + jnp.arange(count, dtype=jnp.int32)
    return 2.0 - 2.0 * jnp.cos(index.astype(jnp.float32) * (2.0 * math.pi / total))


def combine_affine_maps(earlier, later):
    return (later[0] * earlier[0], later[0] * earlier[1] + later[1])


def join_matrices(earlier, later):
    a11, a12, a21, a22 = earlier
    b11, b12, b21, b22 = later
    c11 = b11 * a11 + b12 * a21
    c12 = b11 * a12 + b12 * a22
    c21 = b21 * a11 + b22 * a21
    c22 = b21 * a12 + b22 * a22
    scale = jnp.maximum(
        jnp.maximum(jnp.abs(c11), jnp.abs(c12)), jnp.maximum(jnp.abs(c21), jnp.abs(c22))
    )
    return (c11 / scale, c12 / scale, c21 / scale, c22 / scale)


def solve_chain(fourier_modes, screening, lam):
    planes = fourier_modes.shape[0]
    start = lax.axis_index("gz") * planes
    own = lax.dynamic_slice_in_dim(screening, start, planes)
    diagonals = [2.0 + own[row_index] + lam for row_index in range(planes)]
    unit_array = jnp.ones_like(lam)
    zero_array = jnp.zeros_like(lam)
    matrix = (unit_array, zero_array, zero_array, unit_array)
    for row_index in range(planes):
        matrix = join_matrices(matrix, (zero_array, unit_array, -unit_array, diagonals[row_index]))
    prefix = carried_in(
        matrix, "gz", join_matrices, (unit_array, zero_array, zero_array, unit_array), False
    )
    previous_pivot = prefix[1] / prefix[3]
    pivot_entries = []
    for row_index in range(planes):
        previous_pivot = 1.0 / (diagonals[row_index] - previous_pivot)
        pivot_entries.append(previous_pivot)
    matrix_product = unit_array
    local_elimination = zero_array
    for row_index in range(planes):
        matrix_product = matrix_product * pivot_entries[row_index]
        local_elimination = pivot_entries[row_index] * (
            fourier_modes[row_index] + local_elimination
        )
    prior_rows = carried_in(
        (matrix_product, local_elimination),
        "gz",
        combine_affine_maps,
        (unit_array, zero_array),
        False,
    )
    previous_elimination = prior_rows[1]
    elimination_factors = []
    for row_index in range(planes):
        previous_elimination = pivot_entries[row_index] * (
            fourier_modes[row_index] + previous_elimination
        )
        elimination_factors.append(previous_elimination)
    local_backsweep = zero_array
    for row_index in reversed(range(planes)):
        local_backsweep = (
            elimination_factors[row_index] + pivot_entries[row_index] * local_backsweep
        )
    after = carried_in(
        (matrix_product, local_backsweep), "gz", combine_affine_maps, (unit_array, zero_array), True
    )
    upper_diagonal = after[1]
    values = [None] * planes
    for row_index in reversed(range(planes)):
        upper_diagonal = elimination_factors[row_index] + pivot_entries[row_index] * upper_diagonal
        values[row_index] = upper_diagonal
    return jnp.stack(values)


def local(source, screening):
    highest = lax.Precision.HIGHEST
    table_x = cas_table(NX)
    along_x = jnp.einsum("zyi,ik->zyk", source, table_x, precision=highest)
    columns = lax.all_to_all(along_x, "gy", split_axis=2, concat_axis=1, tiled=True)
    fourier_modes = jnp.einsum("zyx,yl->zlx", columns, table_x, precision=highest)
    width = fourier_modes.shape[2]
    lam = (
        wave_term(0, NY, NY)[:, None] + wave_term(lax.axis_index("gy") * width, width, NX)[None, :]
    )
    solved_rows = solve_chain(fourier_modes, screening, lam)
    back_y = jnp.einsum("zlx,ly->zyx", solved_rows, table_x, precision=highest)
    rows_back = lax.all_to_all(back_y, "gy", split_axis=1, concat_axis=2, tiled=True)
    back_x = jnp.einsum("zyk,kx->zyx", rows_back, table_x, precision=highest)
    return back_x / (NX * NY)


def solution(mesh):
    in_specs = (P("gz", "gy", None), P())
    out_specs = P("gz", "gy", None)
    return jax.shard_map(local, mesh=mesh, in_specs=in_specs, out_specs=out_specs, check_vma=False)
```

profile of v0, /device:TPU:1, one launch (start us, length us, event | category | flops | bytes accessed | tf_op | source)
XLA Modules:
  0.0 1135.8 jit_solution(17158383080362611174)
XLA Ops:
  9.4 1.3 fusion.36
  12.7 5.2 convolution_bitcast_fusion
  18.2 1.3 reshape.291
  19.5 10.2 all-to-all-start
  29.7 6.5 all-to-all-done
  36.8 1.3 reduce
  38.9 5.2 fusion.15
  44.2 71.5 %all-gather.11.cloned.1.call-done = f32[64,512,64]{1,2,0:T(8,128)} async-done(((f32[1,512,64]{1,2,0:T(8,128)}), f32[64,512,64]{1,2,0:T(8,128)}) %all-gather.11.cloned.1.call-update) | async-done | bytes 8388624 | tf_op jit(solution)/shard_map/all_gather | solution.py:14
  115.7 100.5 %all-gather.13.cloned.1.call-done = f32[64,512,64]{1,2,0:T(8,128)} async-done(((f32[1,512,64]{1,2,0:T(8,128)}), f32[64,512,64]{1,2,0:T(8,128)}) %all-gather.13.cloned.1.call-update) | async-done | bytes 8388624 | tf_op jit(solution)/shard_map/all_gather | solution.py:14
  216.2 100.5 %all-gather.15.cloned.1.call-done = f32[64,512,64]{1,2,0:T(8,128)} async-done(((f32[1,512,64]{1,2,0:T(8,128)}), f32[64,512,64]{1,2,0:T(8,128)}) %all-gather.15.cloned.1.call-update) | async-done | bytes 8388624 | tf_op jit(solution)/shard_map/all_gather | solution.py:14
  316.7 100.4 %all-gather.17.cloned.1.call-done = f32[64,512,64]{1,2,0:T(8,128)} async-done(((f32[1,512,64]{1,2,0:T(8,128)}), f32[64,512,64]{1,2,0:T(8,128)}) %all-gather.17.cloned.1.call-update) | async-done | bytes 8388624 | tf_op jit(solution)/shard_map/all_gather | solution.py:14
  417.1 192.2 %while.48 = (s32[]{:T(128)}, f32[512,64]{1,0:T(8,128)S(1)}, f32[512,64]{1,0:T(8,128)S(1)}, f32[512,64]{1,0:T(8,128)S(1)}, f32[512,64]{1,0:T(8,128)S(1)}, /*index...) while((s32[]{:T(128)}, f32[512,64]{1,0:T(8,128)S(1)}, ...), condition=%wide.region_1.2_spmd.clone, body=%wide.region_0.1_spmd.clone.sunk | while | flops 1441796 | bytes 5243027 | solution.py:26
  612.0 96.8 %all-gather.19.cloned.1.call-done = f32[32768,64]{0,1:T(8,128)} async-done(((f32[512,64]{0,1:T(8,128)}), f32[32768,64]{0,1:T(8,128)}) %all-gather.19.cloned.1.call-update) | async-done | bytes 8388624 | tf_op jit(solution)/shard_map/all_gather | solution.py:14
  708.7 12.2 %copy.31 = f32[32768,64]{1,0:T(8,128)} copy(f32[32768,64]{0,1:T(8,128)} %all-gather.19.cloned.1.call-done) | data formatting | bytes 16777216
  720.9 88.1 %all-gather.21.cloned.1.call-done = f32[32768,64]{0,1:T(8,128)} async-done(((f32[512,64]{0,1:T(8,128)}), f32[32768,64]{0,1:T(8,128)}) %all-gather.21.cloned.1.call-update) | async-done | bytes 8388624 | tf_op jit(solution)/shard_map/all_gather | solution.py:14
  809.1 12.2 %copy.29 = f32[32768,64]{1,0:T(8,128)} copy(f32[32768,64]{0,1:T(8,128)} %all-gather.21.cloned.1.call-done) | data formatting | bytes 16777216
  821.3 80.0 %while.49 = (s32[]{:T(128)}, f32[512,64]{1,0:T(8,128)S(1)}, s32[]{:T(128)}, f32[64,512,64]{2,1,0:T(8,128)}, f32[64,512,64]{2,1,0:T(8,128)}, /*index=5*/s32[]{:T(128)}, s32[]{:T(128)}) while((s32[]{:T(128)}, f32[512,64]{1,0:T(8,128)S(1)}, s32[]{:T(128)}, f32[64,512,64]{2,1,0:T(8,128)}, f32[64,512,64]{2,1,0:T(8,128)}, ...), condition=%wide.region_3.4_spmd.clone, body=%wide.region_2.3_spmd.clone.sunk | while | flops 131076 | bytes 524389 | solution.py:26
  822.5 1.2 fusion.64
  823.8 1.2 fusion.64
  827.6 1.2 fusion.64
  831.4 1.2 fusion.64
  835.2 1.2 fusion.64
  839.1 1.2 fusion.64
  842.9 1.2 fusion.64
  846.7 1.2 fusion.64
  847.9 1.2 fusion.64
  851.8 1.2 fusion.64
  855.6 1.2 fusion.64
  859.4 1.2 fusion.64
  863.2 1.2 fusion.64
  867.0 1.2 fusion.64
  870.8 1.2 fusion.64
  872.1 1.2 fusion.64
  875.9 1.2 fusion.64
  879.7 1.2 fusion.64
  883.5 1.2 fusion.64
  887.3 1.2 fusion.64
  891.1 1.2 fusion.64
  895.0 1.2 fusion.64
  896.2 1.2 fusion.64
  900.0 1.2 fusion.64
  902.2 11.5 %rev.6 = f32[64,512,64]{2,1,0:T(8,128)} reverse(f32[64,512,64]{2,1,0:T(8,128)} %get-tuple-element.741), dimensions={0} | reverse | bytes 16777216 | tf_op jit(solution)/shard_map/rev | solution.py:16
  913.7 86.1 %all-gather.23.cloned.1.call-done = f32[32768,64]{0,1:T(8,128)} async-done(((f32[512,64]{0,1:T(8,128)}), f32[32768,64]{0,1:T(8,128)}) %all-gather.23.cloned.1.call-update) | async-done | bytes 8388624 | tf_op jit(solution)/shard_map/all_gather | solution.py:14
  999.8 12.2 %copy.30 = f32[32768,64]{1,0:T(8,128)} copy(f32[32768,64]{0,1:T(8,128)} %all-gather.23.cloned.1.call-done) | data formatting | bytes 16777216 | tf_op jit(solution)/shard_map/all_gather | solution.py:14
  1012.0 11.5 %rev.7 = f32[64,512,64]{2,1,0:T(8,128)} reverse(f32[64,512,64]{2,1,0:T(8,128)} %bitcast.171), dimensions={0} | reverse | bytes 16777216 | tf_op jit(solution)/shard_map/rev | solution.py:16
  1023.5 80.1 %while.50 = (s32[]{:T(128)}, f32[512,64]{1,0:T(8,128)S(1)}, s32[]{:T(128)}, f32[64,512,64]{2,1,0:T(8,128)}, f32[64,512,64]{2,1,0:T(8,128)}, /*index=5*/s32[]{:T(128)}, s32[]{:T(128)}) while((s32[]{:T(128)}, f32[512,64]{1,0:T(8,128)S(1)}, s32[]{:T(128)}, f32[64,512,64]{2,1,0:T(8,128)}, f32[64,512,64]{2,1,0:T(8,128)}, ...), condition=%wide.region_5.6_spmd.clone, body=%wide.region_4.5_spmd.clone.sunk | while | flops 131076 | bytes 524389 | solution.py:26
  1024.8 1.2 fusion.65
  1028.6 1.2 fusion.65
  1032.4 1.2 fusion.65
  1036.2 1.2 fusion.65
  1038.7 1.2 fusion.65
  1042.6 1.2 fusion.65
  1046.4 1.2 fusion.65
  1048.9 1.2 fusion.65
  1052.7 1.2 fusion.65
  1056.5 1.2 fusion.65
  1060.3 1.2 fusion.65
  1062.9 1.2 fusion.65
  1066.7 1.2 fusion.65
  1070.5 1.2 fusion.65
  1103.8 5.2 fusion.14
  1109.9 11.3 all_to_all.36
  1121.1 1.3 reduce.1
  1123.3 5.7 convolution_multiply_fusion
  (702 shorter events, 307.4 us)
Async XLA Ops:
  6.5 6.2 copy-start
  6.5 109.1 %all-gather.11.cloned.1.call-start = ((), (), s32[]{:S(2)}) async-start(), calls=%async_computation.2 | async-start | bytes 8519680 | tf_op jit(solution)/shard_map/all_gather | solution.py:14
  10.7 205.5 %all-gather.13.cloned.1.call-start = ((), (), s32[]{:S(2)}) async-start(), calls=%async_computation.3 | async-start | bytes 8519680 | tf_op jit(solution)/shard_map/all_gather | solution.py:14
  11.4 305.3 %all-gather.15.cloned.1.call-start = ((), (), s32[]{:S(2)}) async-start(), calls=%async_computation.4 | async-start | bytes 8519680 | tf_op jit(solution)/shard_map/all_gather | solution.py:14
  12.2 405.0 %all-gather.17.cloned.1.call-start = ((), (), s32[]{:S(2)}) async-start(), calls=%async_computation.5 | async-start | bytes 8519680 | tf_op jit(solution)/shard_map/all_gather | solution.py:14
  19.5 16.7 %all-to-all-start = ((f32[8,1,8192]{2,1,0:T(1,128)}), f32[8,1,8192]{2,1,0:T(1,128)S(1)}, u32[]{:S(2)}, u32[]{:S(2)}) async-start(f32[8,1,8192]{2,1,0:T(1,128)} %reshape.291), calls=%async_computation | async-start | bytes 524288 | tf_op jit(solution)/shard_map/all_to_all | solution.py:117
  29.7 679.1 %all-gather.19.cloned.1.call-start = ((), (), s32[]{:S(2)}) async-start(), calls=%async_computation.6 | async-start | bytes 8519680 | tf_op jit(solution)/shard_map/all_gather | solution.py:14
  611.1 197.9 %all-gather.21.cloned.1.call-start = ((), (), s32[]{:S(2)}) async-start(), calls=%async_computation.7 | async-start | bytes 8519680 | tf_op jit(solution)/shard_map/all_gather | solution.py:14
  611.7 388.1 %all-gather.23.cloned.1.call-start = ((), (), s32[]{:S(2)}) async-start(), calls=%async_computation.8 | async-start | bytes 8519680 | tf_op jit(solution)/shard_map/all_gather | solution.py:14
  1103.5 25.4 %copy-start.1 = (f32[2,64,512]{2,1,0:T(8,128)S(1)}, f32[2,64,512]{2,1,0:T(8,128)}, u32[]{:S(2)}) copy-start(f32[2,64,512]{2,1,0:T(8,128)} %param.8) | copy-start | bytes 786436
Sparse Core Ops, SparseCore 0:
  10.8 104.8 all-gather.10
  118.7 97.4 all-gather.12
  219.3 97.4 all-gather.14
  319.7 97.4 all-gather.16
  611.3 97.4 all-gather.18
  711.6 97.4 all-gather.20
  902.3 97.4 all-gather.22
where the time goes:
time: 1140 us
  waiting for transfers between devices  653 us (57%)
  local copies, waits for them, and re-layouts  223 us (20%)
  other arithmetic  193 us (17%)
  matrix products  21.4 us (2%)
  between operations  15 us (1%)
    all_gather x7, waiting for transfers between devices, carried_in(): pieces = jax.tree.map(lambda part: lax.all_gather(part, axis), value)  644 us
    select_n x252, other arithmetic, lap(): jnp.where(position < mine, new, old)  187 us
    dynamic_slice x378, local copies, waits for them, and re-layouts, lap(): longer = join(so_far, jax.tree.map(lambda part: part[position], pieces))  156 us
    unnamed x10, local copies, waits for them, and re-layouts  27 us
    rev x2, local copies, waits for them, and re-layouts, carried_in(): pieces = jax.tree.map(lambda part: part[::-1], pieces)  23 us
  transfers between devices with their start and end apart: 8, of which 8 were waited for; matrix products, arithmetic and copies ran while one was open for 3% of the time, Pallas kernels for 0%

commit v1 on v0

v1 whole, which is shorter than its diff:
```python
import math

import jax
import jax.numpy as jnp
import ml_dtypes
import numpy as np
from jax import lax
from jax.experimental import pallas as pl
from jax.experimental.pallas import tpu as pltpu
from jax.sharding import PartitionSpec as P

NX = 512
NY = 512
NZ = 128
HALF = 256
CHUNKS = 8
RUN = NZ // CHUNKS
LINES = 8
PEERS = 64

F32 = jnp.float32
BF16 = jnp.bfloat16


def split_table(table):
    high = table.astype(ml_dtypes.bfloat16)
    low = (table - high.astype(np.float64)).astype(ml_dtypes.bfloat16)
    return np.concatenate([high, low], axis=0)


def cas(rows, columns, total):
    angle = (rows[:, None] * columns[None, :] % total) * (2.0 * math.pi / total)
    return np.cos(angle) + np.sin(angle)


def half_tables():
    index = np.arange(HALF)
    even = cas(2 * index, index, 2 * HALF)
    odd = cas(2 * index + 1, index, 2 * HALF)
    return split_table(even), split_table(odd), split_table(odd.T)


def wave_terms():
    index = np.concatenate([np.arange(0, 512, 2), np.arange(1, 512, 2)])
    return (4.0 * np.sin(index * (math.pi / 512)) ** 2).astype(np.float32)


def split(values):
    high = values.astype(BF16)
    low = (values - high.astype(F32)).astype(BF16)
    return high, low


def times_table(values, table_ref):
    rows = values.shape[0]
    high, low = split(values)
    both = jnp.concatenate([high, low], axis=0)
    main = jnp.dot(both, table_ref[:HALF], preferred_element_type=F32)
    rest = jnp.dot(high, table_ref[HALF:], preferred_element_type=F32)
    return main[:rows] + (main[rows:] + rest)


def table_times_transposed(table_ref, values):
    rows = values.shape[0]
    high, low = split(values)
    both = jnp.concatenate([high, low], axis=0)
    product = lax.dot_general(
        table_ref[...], both, (((1,), (1,)), ((), ())), preferred_element_type=F32
    )
    return product[:HALF, :rows] + (product[:HALF, rows:] + product[HALF:, :rows])


def forward_x_kernel(source_ref, even_ref, odd_ref, out_ref):
    rows = source_ref[...].reshape(128, NX)
    low, high = rows[:, :HALF], rows[:, HALF:]
    out_ref[:HALF] = table_times_transposed(even_ref, low + high)
    out_ref[HALF:] = table_times_transposed(odd_ref, low - high)


def pivots_kernel(place_ref, screening_ref, wave_k_ref, wave_l_ref, pivot_ref, up_ref, down_ref, far_ref, close_ref, state_ref):
    chunk, group = place_ref[0], place_ref[1]
    line = lax.broadcasted_iota(jnp.int32, (LINES, NY), 0)
    lam = jnp.zeros((LINES, NY), F32) + wave_l_ref[...]
    for k in range(LINES):
        lam = lam + jnp.where(line == k, wave_k_ref[group * LINES + k], 0.0)
    one = jnp.ones((LINES, NY), F32)

    def step(plane, total, rise):
        rise = rise + (screening_ref[plane] + lam) * total
        return total + rise, rise

    def lap(index, state):
        below, above = state
        other = CHUNKS - 1 - index

        @pl.when(index == chunk)
        def _():
            state_ref[0] = below

        @pl.when(other == chunk)
        def _():
            state_ref[1] = above

        low_total, low_rise, high_total, high_rise = one, below, one, above
        for t in range(RUN):
            low_total, low_rise = step(index * RUN + t, low_total, low_rise)
            high_total, high_rise = step(other * RUN + RUN - 1 - t, high_total, high_rise)
        low_inverse, high_inverse = 1.0 / low_total, 1.0 / high_total

        @pl.when(index < chunk)
        def _():
            far_ref[index] = low_inverse

        @pl.when(other > chunk)
        def _():
            far_ref[other] = high_inverse

        return low_rise * low_inverse, high_rise * high_inverse

    far_ref[chunk] = jnp.zeros((LINES, NY), F32)
    lax.fori_loop(0, CHUNKS, lap, (one, one))

    first = chunk * RUN
    total, rise = one, state_ref[0]
    for t in range(RUN):
        up_ref[t] = total
        before = total
        total, rise = step(first + t, total, rise)
        pivot_ref[t] = before / total
    inverse = 1.0 / total
    last_pivot = pivot_ref[RUN - 1]
    close_ref[...] = 1.0 / (rise * inverse + last_pivot * state_ref[1])
    for t in range(RUN):
        up_ref[t] = up_ref[t] * inverse

    total, rise = one, state_ref[1]
    for t in reversed(range(RUN)):
        down_ref[t] = total
        total, rise = step(first + t, total, rise)
    inverse = 1.0 / total
    for t in range(RUN):
        down_ref[t] = down_ref[t] * inverse


def swap_halves(values):
    shape = values.shape
    return pltpu.roll(values.reshape(-1, 128), 64, 1).reshape(shape)


def lower_half(shape):
    return lax.broadcasted_iota(jnp.int32, shape, len(shape) - 1) < 64


def forward_y_kernel(place_ref, rows_ref, even_ref, odd_t_ref, up_ref, down_ref, modes_ref, send_ref):
    chunk = place_ref[0]
    blocks = rows_ref[...].reshape(8, 8, LINES, 128)
    keep = lower_half((8, LINES, 128))

    def gather(parts):
        columns = []
        for pair in range(2):
            a, b = parts[2 * pair], parts[2 * pair + 1]
            first = jnp.where(keep, a, swap_halves(b))
            second = jnp.where(keep, swap_halves(a), b)
            columns.append(jnp.stack([first, second], axis=1).reshape(128, 128))
        return jnp.concatenate(columns, axis=1)

    sums = gather([blocks[:, g] + blocks[:, g + 4] for g in range(4)])
    differences = gather([blocks[:, g] - blocks[:, g + 4] for g in range(4)])
    modes_ref[:, :, :HALF] = times_table(sums, even_ref).reshape(RUN, LINES, HALF)
    modes_ref[:, :, HALF:] = times_table(differences, odd_t_ref).reshape(RUN, LINES, HALF)

    upward = jnp.zeros((LINES, NY), F32)
    downward = jnp.zeros((LINES, NY), F32)
    for t in range(RUN):
        plane = modes_ref[t]
        upward = upward + up_ref[t] * plane
        downward = downward + down_ref[t] * plane
    for other in range(CHUNKS):
        send_ref[other] = jnp.where(other > chunk, upward, downward)


def solve_kernel(place_ref, modes_ref, arrived_ref, pivot_ref, far_ref, close_ref, even_ref, odd_ref, out_ref, solved_ref):
    chunk = place_ref[0]
    below = jnp.zeros((LINES, NY), F32)
    above = jnp.zeros((LINES, NY), F32)
    for other in range(CHUNKS):
        below = jnp.where(other < chunk, arrived_ref[other] + far_ref[other] * below, below)
        rest = CHUNKS - 1 - other
        above = jnp.where(rest > chunk, arrived_ref[rest] + far_ref[rest] * above, above)

    elimination = below
    for t in range(RUN):
        elimination = pivot_ref[t] * (modes_ref[t] + elimination)
        solved_ref[t] = elimination
    value = (elimination + pivot_ref[RUN - 1] * above) * close_ref[...]
    solved_ref[RUN - 1] = value
    for t in reversed(range(RUN - 1)):
        value = solved_ref[t] + pivot_ref[t] * value
        solved_ref[t] = value

    solved = solved_ref[...].reshape(128, NY)
    even = times_table(solved[:, :HALF], even_ref)
    odd = times_table(solved[:, HALF:], odd_ref)
    keep = lower_half((8, LINES, 128))
    for base, values in ((0, even + odd), (4, even - odd)):
        for pair in range(2):
            column = values[:, pair * 128 : pair * 128 + 128].reshape(8, 2, LINES, 128)
            a, b = column[:, 0], column[:, 1]
            out_ref[:, base + 2 * pair] = jnp.where(keep, a, swap_halves(b))
            out_ref[:, base + 2 * pair + 1] = jnp.where(keep, swap_halves(a), b)


def backward_x_kernel(rows_ref, even_ref, odd_ref, out_ref):
    values = rows_ref[...].T
    even = times_table(values[:, :HALF], even_ref)
    odd = times_table(values[:, HALF:], odd_ref)
    scale = 1.0 / (NX * NY)
    out_ref[:, :, :HALF] = ((even + odd) * scale).reshape(2, 64, HALF)
    out_ref[:, :, HALF:] = ((even - odd) * scale).reshape(2, 64, HALF)


VMEM = pl.BlockSpec(memory_space=pltpu.VMEM)
SMEM = pl.BlockSpec(memory_space=pltpu.SMEM)


def call(kernel, ins, outs, scratch=(), name=None):
    return pl.pallas_call(
        kernel,
        in_specs=ins,
        out_specs=jax.tree.map(lambda _: VMEM, outs),
        out_shape=outs,
        scratch_shapes=list(scratch),
        compiler_params=pltpu.CompilerParams(vmem_limit_bytes=16 * 1024 * 1024),
        name=name,
    )


def shape(*sizes):
    return jax.ShapeDtypeStruct(sizes, F32)


RUN_PEERS = [[run * PEERS + peer for peer in range(PEERS)] for run in range(CHUNKS)]
RUNS = [[run * 8 + y for run in range(CHUNKS)] for y in range(8)]


def exchange_peers(values):
    pieces = values.reshape(PEERS, LINES, 128)
    pieces = lax.all_to_all(
        pieces, ("gz", "gy"), 0, 0, tiled=True, axis_index_groups=RUN_PEERS
    )
    return pieces.reshape(512, 128)


def local(source, screening):
    even, odd, odd_t = (jnp.asarray(table) for table in half_tables())
    waves = wave_terms()
    gz, gy = lax.axis_index("gz"), lax.axis_index("gy")
    place = jnp.stack([gz // 8, (gz % 8) * 8 + gy]).astype(jnp.int32)

    along_x = call(forward_x_kernel, [VMEM] * 3, shape(512, 128), name="forward_x")(
        source, even, odd
    )
    columns = exchange_peers(along_x)
    planes = shape(RUN, LINES, NY)
    pivots, up, down, far, close = call(
        pivots_kernel,
        [SMEM, SMEM, SMEM, VMEM],
        (planes, planes, planes, shape(CHUNKS, LINES, NY), shape(LINES, NY)),
        [pltpu.VMEM((2, LINES, NY), F32)],
        name="pivots",
    )(place, screening, jnp.asarray(waves), jnp.asarray(waves)[None, :])
    modes, send = call(
        forward_y_kernel,
        [SMEM] + [VMEM] * 5,
        (planes, shape(CHUNKS, LINES, NY)),
        name="forward_y",
    )(place, columns, even, odd_t, up, down)
    arrived = lax.all_to_all(send, "gz", 0, 0, tiled=True, axis_index_groups=RUNS)
    back_y = call(
        solve_kernel,
        [SMEM] + [VMEM] * 7,
        shape(8, 8, LINES, 128),
        [pltpu.VMEM((RUN, LINES, NY), F32)],
        name="solve",
    )(place, modes, arrived, pivots, far, close, even, odd)
    rows = exchange_peers(back_y)
    return call(backward_x_kernel, [VMEM] * 3, shape(2, 64, NX), name="backward_x")(
        rows, even, odd
    )


def solution(mesh):
    in_specs = (P("gz", "gy", None), P())
    out_specs = P("gz", "gy", None)
    return jax.shard_map(local, mesh=mesh, in_specs=in_specs, out_specs=out_specs, check_vma=False)
```

time: 1140 us -> 69.3 us (0.06)
  waiting for transfers between devices: 653 us -> 10.9 us
  local copies, waits for them, and re-layouts: 223 us -> 3.47 us
  other arithmetic: 193 us -> 0.08 us
  blocking collectives: 11.3 us -> 37.1 us
  matrix products: 21.4 us -> 0 us
  between operations: 15 us -> 0.1 us
    all_gather x7 -> x0, waiting for transfers between devices: 644 us -> none  [carried_in(): pieces = jax.tree.map(lambda part: lax.all_gather(part, axis), value)]
    select_n x252 -> x0, other arithmetic: 187 us -> none  [lap(): jnp.where(position < mine, new, old)]
    dynamic_slice x379 -> x0, local copies, waits for them, and re-layouts: 157 us -> none  [the longest x378 156 us: lap(): longer = join(so_far, jax.tree.map(lambda part: part[position], pieces))]
    all_to_all x1 -> x2, blocking collectives: 11.3 us -> 37.1 us  [the longest x1 19 us: exchange_peers(): lax.all_to_all(pieces, ('gz', 'gy'), 0, 0, tiled=True, axis_index_groups=...]
    unnamed x10 -> x18, local copies, waits for them, and re-layouts: 27 us -> 3.47 us
    rev x2 -> x0, local copies, waits for them, and re-layouts: 23 us -> none  [carried_in(): pieces = jax.tree.map(lambda part: part[::-1], pieces)]
    all_gather x1 -> x0, local copies, waits for them, and re-layouts: 12.2 us -> none  [carried_in(): pieces = jax.tree.map(lambda part: lax.all_gather(part, axis), value)]
  transfers between devices with their start and end apart: 8 -> 1, of which waited for: 8 -> 1; matrix products, arithmetic and copies ran while one was open for 3% -> 0% of each run, Pallas kernels for 0% -> 2%
where the time goes in v1:
time: 69.3 us; the launch traced here: 68.9 us
  blocking collectives  37.1 us (54%)
  starting transfers between devices  11.7 us (17%)
  waiting for transfers between devices  10.9 us (16%)
  Pallas kernels  5.54 us (8%)
  local copies, waits for them, and re-layouts  3.47 us (5%)
    all_to_all x1, blocking collectives, exchange_peers(): lax.all_to_all(pieces, ('gz', 'gy'), 0, 0, tiled=True, axis_index_groups=...  19 us
    all_to_all x1, blocking collectives, local(): lax.all_to_all(send, 'gz', 0, 0, tiled=True, axis_index_groups=RUNS)  18.1 us
    all_to_all x1, starting transfers between devices, exchange_peers(): lax.all_to_all(pieces, ('gz', 'gy'), 0, 0, tiled=True, axis_index_groups=...  11.7 us
    all_to_all x1, waiting for transfers between devices, exchange_peers(): lax.all_to_all(pieces, ('gz', 'gy'), 0, 0, tiled=True, axis_index_groups=...  10.9 us
    unnamed x18, local copies, waits for them, and re-layouts  3.47 us
    pallas_call x1, Pallas kernels, local(): call(pivots_kernel, [SMEM, SMEM, SMEM, VMEM], (planes, planes, planes, sh...  1.55 us
  transfers between devices with their start and end apart: 1, of which 1 were waited for; matrix products, arithmetic and copies ran while one was open for 0% of the time, Pallas kernels for 2%

profile of v1, /device:TPU:1, one launch (start us, length us, event | category | flops | bytes accessed | tf_op | source)
XLA Modules:
  0.0 68.9 jit_solution(11760261690863076084)
XLA Ops:
  0.0 0.0 copy-start
  0.0 0.9 %copy-done = bf16[512,256]{1,0:T(8,128)(2,1)S(1)} copy-done((bf16[512,256]{1,0:T(8,128)(2,1)S(1)}, bf16[512,256]{1,0:T(8,128)(2,1)}, u32[]{:S(2)}) %copy-start) | copy-done | bytes 262168
  1.0 0.0 copy-start.2
  1.0 0.9 %copy-done.2 = bf16[512,256]{1,0:T(8,128)(2,1)S(1)} copy-done((bf16[512,256]{1,0:T(8,128)(2,1)S(1)}, bf16[512,256]{1,0:T(8,128)(2,1)}, u32[]{:S(2)}) %copy-start.2) | copy-done | bytes 262168
  1.9 0.0 copy-start.5
  1.9 0.9 %copy-done.5 = f32[2,64,512]{2,1,0:T(8,128)S(1)} copy-done((f32[2,64,512]{2,1,0:T(8,128)S(1)}, f32[2,64,512]{2,1,0:T(8,128)}, u32[]{:S(2)}) %copy-start.5) | copy-done | bytes 262168
  2.9 1.0 %forward_x.1 = f32[512,128]{1,0:T(8,128)} custom-call(f32[2,64,512]{2,1,0:T(8,128)S(1)} %copy-done.5, bf16[512,256]{1,0:T(8,128)(2,1)S(1)} %copy-done, bf16[512,256]{1,0:T(8,128)(2,1)S(1)} %copy-done.2), custom_call_target="tpu_custom_call" | custom-call | tf_op jit(solution)/shard_map/forward_x/pallas_call | solution.py:261
  3.9 0.0 copy-start.1
  3.9 0.0 copy-start.4
  3.9 11.7 %all-to-all-start = ((f32[64,8,128]{2,1,0:T(8,128)}), f32[64,8,128]{2,1,0:T(8,128)S(1)}, u32[]{:S(2)}, u32[]{:S(2)}) async-start(f32[64,8,128]{2,1,0:T(8,128)} %bitcast.2), calls=%async_computation | async-start | bytes 524288 | tf_op jit(solution)/shard_map/all_to_all | solution.py:249
  15.7 0.0 copy-start.7
  15.7 0.0 copy-start.6
  15.7 0.0 copy-start.8
  15.7 0.1 pad_add_fusion.place_ref
  15.8 0.6 copy-done.7
  16.4 0.0 copy-done.6
  16.4 0.0 copy-done.8
  16.4 1.6 %pivots.1 = (f32[16,8,512]{2,1,0:T(8,128)S(1)}, f32[16,8,512]{2,1,0:T(8,128)S(1)}, f32[16,8,512]{2,1,0:T(8,128)S(1)}, f32[8,8,512]{2,1,0:T(8,128)S(1)}, f32[8,512]{1,0:T(8,128)S(1)}) custom-call(s32[2]{0:T(128)S(1)} %pad_add_fusion.place_ref, f32[128]{0:T(128)S(1)} %copy-done.8, f32[512]{0:T(512)S(1)} %copy-done.7, f32[1,512]{1,0:T(1,128)S(1)} %copy-done.6), custom_call_target="tpu_custom_call" | custom-call | tf_op jit(solution)/shard_map/pivots/pallas_call | solution.py:266
  17.9 10.9 %all-to-all-done = f32[64,8,128]{2,1,0:T(8,128)S(1)} async-done(((f32[64,8,128]{2,1,0:T(8,128)}), f32[64,8,128]{2,1,0:T(8,128)S(1)}, u32[]{:S(2)}, u32[]{:S(2)}) %all-to-all-start) | async-done | bytes 262176 | tf_op jit(solution)/shard_map/all_to_all | solution.py:249
  28.8 0.0 copy-done.1
  28.8 0.0 copy-done.4
  28.8 0.9 %forward_y.1 = (f32[16,8,512]{2,1,0:T(8,128)S(1)}, f32[8,8,512]{2,1,0:T(8,128)S(1)}) custom-call(s32[2]{0:T(128)S(1)} %pad_add_fusion.place_ref, f32[512,128]{1,0:T(8,128)S(1)} %bitcast.6, bf16[512,256]{1,0:T(8,128)(2,1)S(1)} %copy-done.1, bf16[512,256]{1,0:T(8,128)(2,1)S(1)} %copy-done.4, f32[16,8,512]{2,1,0:T(8,128)S(1)} %get-tuple-element.12.up_ref, ...), custom_call_target="tpu_custom_call" | custom-call | tf_op jit(solution)/shard_map/forward_y/pallas_call | solution.py:273
  29.7 0.0 copy-start.3
  29.7 18.1 %all_to_all.15.arrived_ref = f32[8,8,512]{2,1,0:T(8,128)S(1)} all-to-all(f32[8,8,512]{2,1,0:T(8,128)S(1)} %get-tuple-element.15), channel_id=1, replica_groups={{0,64,128,192,256,320,384,448},{8,72,136,200,264,328,392,456},{16,80,14..., dimensions={0} | all-to-all | bytes 262144 | tf_op jit(solution)/shard_map/all_to_all | solution.py:279
  47.8 0.0 copy-done.3
  47.8 1.0 %solve.1 = f32[8,8,8,128]{3,2,1,0:T(8,128)S(1)} custom-call(s32[2]{0:T(128)S(1)} %pad_add_fusion.place_ref, f32[16,8,512]{2,1,0:T(8,128)S(1)} %get-tuple-element.14.modes_ref, f32[8,8,512]{2,1,0:T(8,128)S(1)} %all_to_all.15.arrived_ref, f32[16,8,512]{2,1,0:T(8,128)S(1)} %get-tuple-element.16.pivot_ref, f32[8,8,512]{2,1,0:T(8,128)S(1)} %get-tuple-element.17.far_ref, ...), custom_call_target="tpu_custom_call" | custom-call | tf_op jit(solution)/shard_map/solve/pallas_call | solution.py:280
  48.9 19.0 %all_to_all.16 = f32[64,8,128]{2,1,0:T(8,128)S(1)} all-to-all(f32[64,8,128]{2,1,0:T(8,128)S(1)} %bitcast.7), channel_id=1, replica_groups={{0,1,2,3,4,5,6,7,8,9,10,11,12,13,14,15,16,17,18,19,20,21,22,23,24,25,26..., dimensions={0} | all-to-all | bytes 524288 | tf_op jit(solution)/shard_map/all_to_all | solution.py:249
  67.9 1.0 %backward_x.1 = f32[2,64,512]{2,1,0:T(8,128)} custom-call(f32[512,128]{1,0:T(8,128)S(1)} %bitcast.8, bf16[512,256]{1,0:T(8,128)(2,1)S(1)} %copy-done.1, bf16[512,256]{1,0:T(8,128)(2,1)S(1)} %copy-done.3), custom_call_target="tpu_custom_call" | custom-call | tf_op jit(solution)/shard_map/backward_x/pallas_call | solution.py:288
Async XLA Ops:
  0.0 0.9 %copy-start = (bf16[512,256]{1,0:T(8,128)(2,1)S(1)}, bf16[512,256]{1,0:T(8,128)(2,1)}, u32[]{:S(2)}) copy-start(bf16[512,256]{1,0:T(8,128)(2,1)} %constant.43.clone.even_ref) | copy-start | bytes 786436
  1.0 0.9 %copy-start.2 = (bf16[512,256]{1,0:T(8,128)(2,1)S(1)}, bf16[512,256]{1,0:T(8,128)(2,1)}, u32[]{:S(2)}) copy-start(bf16[512,256]{1,0:T(8,128)(2,1)} %constant.44.clone.odd_ref) | copy-start | bytes 786436
  1.9 0.9 %copy-start.5 = (f32[2,64,512]{2,1,0:T(8,128)S(1)}, f32[2,64,512]{2,1,0:T(8,128)}, u32[]{:S(2)}) copy-start(f32[2,64,512]{2,1,0:T(8,128)} %source_ref.1) | copy-start | bytes 786436
  3.9 24.9 %copy-start.1 = (bf16[512,256]{1,0:T(8,128)(2,1)S(1)}, bf16[512,256]{1,0:T(8,128)(2,1)}, u32[]{:S(2)}) copy-start(bf16[512,256]{1,0:T(8,128)(2,1)} %constant.43.clone.even_ref) | copy-start | bytes 786436
  3.9 24.9 %copy-start.4 = (bf16[512,256]{1,0:T(8,128)(2,1)S(1)}, bf16[512,256]{1,0:T(8,128)(2,1)}, u32[]{:S(2)}) copy-start(bf16[512,256]{1,0:T(8,128)(2,1)} %constant.45.clone.odd_t_ref) | copy-start | bytes 786436
  3.9 24.9 %all-to-all-start = ((f32[64,8,128]{2,1,0:T(8,128)}), f32[64,8,128]{2,1,0:T(8,128)S(1)}, u32[]{:S(2)}, u32[]{:S(2)}) async-start(f32[64,8,128]{2,1,0:T(8,128)} %bitcast.2), calls=%async_computation | async-start | bytes 524288 | tf_op jit(solution)/shard_map/all_to_all | solution.py:249
  15.7 0.7 copy-start.7
  15.7 0.7 copy-start.6
  15.7 0.7 copy-start.8
  29.7 18.1 %copy-start.3 = (bf16[512,256]{1,0:T(8,128)(2,1)S(1)}, bf16[512,256]{1,0:T(8,128)(2,1)}, u32[]{:S(2)}) copy-start(bf16[512,256]{1,0:T(8,128)(2,1)} %constant.44.clone.odd_ref) | copy-start | bytes 786436

commit v2 on v1

--- a/solution.py
+++ b/solution.py
@@ -17,6 +17,8 @@
 RUN = NZ // CHUNKS
 LINES = 8
 PEERS = 64
+FIRST_RUN = 4
+FIRST_Y = 4
 
 F32 = jnp.float32
 BF16 = jnp.bfloat16
@@ -70,7 +72,24 @@
     return product[:HALF, :rows] + (product[:HALF, rows:] + product[HALF:, :rows])
 
 
-def forward_x_kernel(source_ref, even_ref, odd_ref, out_ref):
+def row(plane):
+    return (plane - 2 * FIRST_Y) % RUN
+
+
+def place_of_run(run):
+    return (run - FIRST_RUN) % CHUNKS
+
+
+def forward_x_kernel(source_hbm, even_hbm, odd_hbm, out_ref, source_ref, even_ref, odd_ref, arrived):
+    copies = [
+        pltpu.make_async_copy(source_hbm, source_ref, arrived.at[0]),
+        pltpu.make_async_copy(even_hbm, even_ref, arrived.at[1]),
+        pltpu.make_async_copy(odd_hbm, odd_ref, arrived.at[2]),
+    ]
+    for copy in copies:
+        copy.start()
+    for copy in copies:
+        copy.wait()
     rows = source_ref[...].reshape(128, NX)
     low, high = rows[:, :HALF], rows[:, HALF:]
     out_ref[:HALF] = table_times_transposed(even_ref, low + high)
@@ -173,11 +192,11 @@
     upward = jnp.zeros((LINES, NY), F32)
     downward = jnp.zeros((LINES, NY), F32)
     for t in range(RUN):
-        plane = modes_ref[t]
+        plane = modes_ref[row(t)]
         upward = upward + up_ref[t] * plane
         downward = downward + down_ref[t] * plane
     for other in range(CHUNKS):
-        send_ref[other] = jnp.where(other > chunk, upward, downward)
+        send_ref[place_of_run(other)] = jnp.where(other > chunk, upward, downward)
 
 
 def solve_kernel(place_ref, modes_ref, arrived_ref, pivot_ref, far_ref, close_ref, even_ref, odd_ref, out_ref, solved_ref):
@@ -185,19 +204,19 @@
     below = jnp.zeros((LINES, NY), F32)
     above = jnp.zeros((LINES, NY), F32)
     for other in range(CHUNKS):
-        below = jnp.where(other < chunk, arrived_ref[other] + far_ref[other] * below, below)
+        below = jnp.where(other < chunk, arrived_ref[place_of_run(other)] + far_ref[other] * below, below)
         rest = CHUNKS - 1 - other
-        above = jnp.where(rest > chunk, arrived_ref[rest] + far_ref[rest] * above, above)
+        above = jnp.where(rest > chunk, arrived_ref[place_of_run(rest)] + far_ref[rest] * above, above)
 
     elimination = below
     for t in range(RUN):
-        elimination = pivot_ref[t] * (modes_ref[t] + elimination)
-        solved_ref[t] = elimination
+        elimination = pivot_ref[t] * (modes_ref[row(t)] + elimination)
+        solved_ref[row(t)] = elimination
     value = (elimination + pivot_ref[RUN - 1] * above) * close_ref[...]
-    solved_ref[RUN - 1] = value
+    solved_ref[row(RUN - 1)] = value
     for t in reversed(range(RUN - 1)):
-        value = solved_ref[t] + pivot_ref[t] * value
-        solved_ref[t] = value
+        value = solved_ref[row(t)] + pivot_ref[t] * value
+        solved_ref[row(t)] = value
 
     solved = solved_ref[...].reshape(128, NY)
     even = times_table(solved[:, :HALF], even_ref)
@@ -221,17 +240,18 @@
 
 
 VMEM = pl.BlockSpec(memory_space=pltpu.VMEM)
+HBM = pl.BlockSpec(memory_space=pltpu.HBM)
 SMEM = pl.BlockSpec(memory_space=pltpu.SMEM)
 
 
-def call(kernel, ins, outs, scratch=(), name=None):
+def call(kernel, ins, outs, scratch=(), name=None, limit=16 * 1024 * 1024):
     return pl.pallas_call(
         kernel,
         in_specs=ins,
         out_specs=jax.tree.map(lambda _: VMEM, outs),
         out_shape=outs,
         scratch_shapes=list(scratch),
-        compiler_params=pltpu.CompilerParams(vmem_limit_bytes=16 * 1024 * 1024),
+        compiler_params=pltpu.CompilerParams(vmem_limit_bytes=limit),
         name=name,
     )
 
@@ -240,8 +260,10 @@
     return jax.ShapeDtypeStruct(sizes, F32)
 
 
-RUN_PEERS = [[run * PEERS + peer for peer in range(PEERS)] for run in range(CHUNKS)]
-RUNS = [[run * 8 + y for run in range(CHUNKS)] for y in range(8)]
+RUN_PEERS = [
+    [run * PEERS + (peer + FIRST_Y * 8) % PEERS for peer in range(PEERS)] for run in range(CHUNKS)
+]
+RUNS = [[(run + FIRST_RUN) % CHUNKS * 8 + y for run in range(CHUNKS)] for y in range(8)]
 
 
 def exchange_peers(values):
@@ -256,11 +278,21 @@
     even, odd, odd_t = (jnp.asarray(table) for table in half_tables())
     waves = wave_terms()
     gz, gy = lax.axis_index("gz"), lax.axis_index("gy")
-    place = jnp.stack([gz // 8, (gz % 8) * 8 + gy]).astype(jnp.int32)
-
-    along_x = call(forward_x_kernel, [VMEM] * 3, shape(512, 128), name="forward_x")(
-        source, even, odd
-    )
+    place = jnp.stack([gz // 8, (gz + 8 - FIRST_Y) % 8 * 8 + gy]).astype(jnp.int32)
+
+    along_x = call(
+        forward_x_kernel,
+        [HBM] * 3,
+        shape(512, 128),
+        [
+            pltpu.VMEM((2, 64, NX), F32),
+            pltpu.VMEM((2 * HALF, HALF), BF16),
+            pltpu.VMEM((2 * HALF, HALF), BF16),
+            pltpu.SemaphoreType.DMA((3,)),
+        ],
+        name="forward_x",
+        limit=60 * 1024 * 1024,
+    )(source, even, odd)
     columns = exchange_peers(along_x)
     planes = shape(RUN, LINES, NY)
     pivots, up, down, far, close = call(

time: 69.3 us -> 61.6 us (0.89)
  waiting for transfers between devices: 10.9 us -> 6.41 us
  blocking collectives: 37.1 us -> 32.9 us
  local copies, waits for them, and re-layouts: 3.47 us -> 0.62 us
  starting transfers between devices: 11.7 us -> 14.5 us
  Pallas kernels: 5.54 us -> 6.67 us
    all_to_all x1, waiting for transfers between devices: 10.9 us -> 6.41 us  [exchange_peers(): lax.all_to_all(pieces, ('gz', 'gy'), 0, 0, tiled=True, axis_index_groups=...]
    all_to_all x1, blocking collectives: 18.1 us -> 13.8 us  [local(): lax.all_to_all(send, 'gz', 0, 0, tiled=True, axis_index_groups=RUNS)]
    unnamed x18 -> x12, local copies, waits for them, and re-layouts: 3.47 us -> 0.62 us
    all_to_all x1, starting transfers between devices: 11.7 us -> 14.5 us  [exchange_peers(): lax.all_to_all(pieces, ('gz', 'gy'), 0, 0, tiled=True, axis_index_groups=...]
    pallas_call x1, Pallas kernels: 1.04 us -> 2.17 us  [local(): call(forward_x_kernel, [HBM] * 3, shape(512, 128), [pltpu.VMEM((2, 64, NX...]
  transfers between devices with their start and end apart: 1 -> 1, of which waited for: 1 -> 1; matrix products, arithmetic and copies ran while one was open for 0% -> 0% of each run, Pallas kernels for 2% -> 3%
where the time goes in v2:
time: 61.6 us; the launch traced here: 61.3 us
  blocking collectives  32.9 us (53%)
  starting transfers between devices  14.5 us (24%)
  Pallas kernels  6.67 us (11%)
  waiting for transfers between devices  6.41 us (10%)
  local copies, waits for them, and re-layouts  0.62 us (1%)
    all_to_all x1, blocking collectives, exchange_peers(): lax.all_to_all(pieces, ('gz', 'gy'), 0, 0, tiled=True, axis_index_groups=...  19.1 us
    all_to_all x1, starting transfers between devices, exchange_peers(): lax.all_to_all(pieces, ('gz', 'gy'), 0, 0, tiled=True, axis_index_groups=...  14.5 us
    all_to_all x1, blocking collectives, local(): lax.all_to_all(send, 'gz', 0, 0, tiled=True, axis_index_groups=RUNS)  13.8 us
    all_to_all x1, waiting for transfers between devices, exchange_peers(): lax.all_to_all(pieces, ('gz', 'gy'), 0, 0, tiled=True, axis_index_groups=...  6.41 us
    pallas_call x1, Pallas kernels, local(): call(forward_x_kernel, [HBM] * 3, shape(512, 128), [pltpu.VMEM((2, 64, NX...  2.17 us
    pallas_call x1, Pallas kernels, local(): call(pivots_kernel, [SMEM, SMEM, SMEM, VMEM], (planes, planes, planes, sh...  1.55 us
  transfers between devices with their start and end apart: 1, of which 1 were waited for; matrix products, arithmetic and copies ran while one was open for 0% of the time, Pallas kernels for 3%

profile of v2, /device:TPU:1, one launch (start us, length us, event | category | flops | bytes accessed | tf_op | source)
XLA Modules:
  0.0 61.3 jit_solution(5879468632509021728)
XLA Ops:
  0.0 2.2 %forward_x.1 = f32[512,128]{1,0:T(8,128)} custom-call(f32[2,64,512]{2,1,0:T(8,128)} %source_hbm.1, bf16[512,256]{1,0:T(8,128)(2,1)} %constant.47.clone.even_hbm.even_ref, bf16[512,256]{1,0:T(8,128)(2,1)} %constant.48.clone.odd_hbm.odd_ref), custom_call_target="tpu_custom_call" | custom-call | tf_op jit(solution)/shard_map/forward_x/pallas_call | solution.py:283
  2.2 0.0 copy-start
  2.2 0.0 copy-start.2
  2.2 14.5 %all-to-all-start = ((f32[64,8,128]{2,1,0:T(8,128)}), f32[64,8,128]{2,1,0:T(8,128)S(1)}, u32[]{:S(2)}, u32[]{:S(2)}) async-start(f32[64,8,128]{2,1,0:T(8,128)} %bitcast.9), calls=%async_computation | async-start | bytes 524288 | tf_op jit(solution)/shard_map/all_to_all | solution.py:271
  16.8 0.0 copy-start.4
  16.8 0.0 copy-start.3
  16.8 0.0 copy-start.5
  16.8 0.1 pad_add_fusion.place_ref
  16.9 0.6 copy-done.4
  17.4 0.0 copy-done.3
  17.5 0.0 copy-done.5
  17.5 1.6 %pivots.1 = (f32[16,8,512]{2,1,0:T(8,128)S(1)}, f32[16,8,512]{2,1,0:T(8,128)S(1)}, f32[16,8,512]{2,1,0:T(8,128)S(1)}, f32[8,8,512]{2,1,0:T(8,128)S(1)}, f32[8,512]{1,0:T(8,128)S(1)}) custom-call(s32[2]{0:T(128)S(1)} %pad_add_fusion.place_ref, f32[128]{0:T(128)S(1)} %copy-done.5, f32[512]{0:T(512)S(1)} %copy-done.4, f32[1,512]{1,0:T(1,128)S(1)} %copy-done.3), custom_call_target="tpu_custom_call" | custom-call | tf_op jit(solution)/shard_map/pivots/pallas_call | solution.py:298
  19.0 6.4 %all-to-all-done = f32[64,8,128]{2,1,0:T(8,128)S(1)} async-done(((f32[64,8,128]{2,1,0:T(8,128)}), f32[64,8,128]{2,1,0:T(8,128)S(1)}, u32[]{:S(2)}, u32[]{:S(2)}) %all-to-all-start) | async-done | bytes 262176 | tf_op jit(solution)/shard_map/all_to_all | solution.py:271
  25.4 0.0 copy-done
  25.4 0.0 copy-done.2
  25.4 0.9 %forward_y.1 = (f32[16,8,512]{2,1,0:T(8,128)S(1)}, f32[8,8,512]{2,1,0:T(8,128)S(1)}) custom-call(s32[2]{0:T(128)S(1)} %pad_add_fusion.place_ref, f32[512,128]{1,0:T(8,128)S(1)} %bitcast.6, bf16[512,256]{1,0:T(8,128)(2,1)S(1)} %copy-done, bf16[512,256]{1,0:T(8,128)(2,1)S(1)} %copy-done.2, f32[16,8,512]{2,1,0:T(8,128)S(1)} %get-tuple-element.12.up_ref, ...), custom_call_target="tpu_custom_call" | custom-call | tf_op jit(solution)/shard_map/forward_y/pallas_call | solution.py:305
  26.3 0.0 copy-start.1
  26.4 13.8 %all_to_all.15.arrived_ref = f32[8,8,512]{2,1,0:T(8,128)S(1)} all-to-all(f32[8,8,512]{2,1,0:T(8,128)S(1)} %get-tuple-element.15), channel_id=1, replica_groups={{256,320,384,448,0,64,128,192},{264,328,392,456,8,72,136,200},{272,336,..., dimensions={0} | all-to-all | bytes 262144 | tf_op jit(solution)/shard_map/all_to_all | solution.py:311
  40.2 0.0 copy-done.1
  40.2 1.0 %solve.1 = f32[8,8,8,128]{3,2,1,0:T(8,128)S(1)} custom-call(s32[2]{0:T(128)S(1)} %pad_add_fusion.place_ref, f32[16,8,512]{2,1,0:T(8,128)S(1)} %get-tuple-element.14.modes_ref, f32[8,8,512]{2,1,0:T(8,128)S(1)} %all_to_all.15.arrived_ref, f32[16,8,512]{2,1,0:T(8,128)S(1)} %get-tuple-element.16.pivot_ref, f32[8,8,512]{2,1,0:T(8,128)S(1)} %get-tuple-element.17.far_ref, ...), custom_call_target="tpu_custom_call" | custom-call | tf_op jit(solution)/shard_map/solve/pallas_call | solution.py:312
  41.2 19.1 %all_to_all.16 = f32[64,8,128]{2,1,0:T(8,128)S(1)} all-to-all(f32[64,8,128]{2,1,0:T(8,128)S(1)} %bitcast.7), channel_id=1, replica_groups={{32,33,34,35,36,37,38,39,40,41,42,43,44,45,46,47,48,49,50,51,52,53,54,5..., dimensions={0} | all-to-all | bytes 524288 | tf_op jit(solution)/shard_map/all_to_all | solution.py:271
  60.3 1.0 %backward_x.1 = f32[2,64,512]{2,1,0:T(8,128)} custom-call(f32[512,128]{1,0:T(8,128)S(1)} %bitcast.8, bf16[512,256]{1,0:T(8,128)(2,1)S(1)} %copy-done, bf16[512,256]{1,0:T(8,128)(2,1)S(1)} %copy-done.1), custom_call_target="tpu_custom_call" | custom-call | tf_op jit(solution)/shard_map/backward_x/pallas_call | solution.py:320
Async XLA Ops:
  2.2 23.3 %copy-start = (bf16[512,256]{1,0:T(8,128)(2,1)S(1)}, bf16[512,256]{1,0:T(8,128)(2,1)}, u32[]{:S(2)}) copy-start(bf16[512,256]{1,0:T(8,128)(2,1)} %constant.47.clone.even_hbm.even_ref) | copy-start | bytes 786436
  2.2 23.2 %copy-start.2 = (bf16[512,256]{1,0:T(8,128)(2,1)S(1)}, bf16[512,256]{1,0:T(8,128)(2,1)}, u32[]{:S(2)}) copy-start(bf16[512,256]{1,0:T(8,128)(2,1)} %constant.49.clone.odd_t_ref) | copy-start | bytes 786436
  2.2 23.2 %all-to-all-start = ((f32[64,8,128]{2,1,0:T(8,128)}), f32[64,8,128]{2,1,0:T(8,128)S(1)}, u32[]{:S(2)}, u32[]{:S(2)}) async-start(f32[64,8,128]{2,1,0:T(8,128)} %bitcast.9), calls=%async_computation | async-start | bytes 524288 | tf_op jit(solution)/shard_map/all_to_all | solution.py:271
  16.8 0.7 %copy-start.4 = (f32[512]{0:T(512)S(1)}, f32[512]{0:T(512)}, u32[]{:S(2)}) copy-start(f32[512]{0:T(512)} %constant.50.clone.wave_k_ref) | copy-start | bytes 6148
  16.8 0.7 %copy-start.3 = (f32[1,512]{1,0:T(1,128)S(1)}, f32[1,512]{1,0:T(1,128)}, u32[]{:S(2)}) copy-start(f32[1,512]{1,0:T(1,128)} %constant.52.wave_l_ref) | copy-start | bytes 6148
  16.8 0.7 %copy-start.5 = (f32[128]{0:T(128)S(1)}, f32[128]{0:T(128)}, u32[]{:S(2)}) copy-start(f32[128]{0:T(128)} %screening_ref.1) | copy-start | bytes 1540
  26.3 13.8 %copy-start.1 = (bf16[512,256]{1,0:T(8,128)(2,1)S(1)}, bf16[512,256]{1,0:T(8,128)(2,1)}, u32[]{:S(2)}) copy-start(bf16[512,256]{1,0:T(8,128)(2,1)} %constant.48.clone.odd_hbm.odd_ref) | copy-start | bytes 786436

commit v3 on v2

--- a/solution.py
+++ b/solution.py
@@ -88,16 +88,18 @@
     ]
     for copy in copies:
         copy.start()
-    for copy in copies:
-        copy.wait()
+    copies[0].wait()
     rows = source_ref[...].reshape(128, NX)
     low, high = rows[:, :HALF], rows[:, HALF:]
+    copies[1].wait()
     out_ref[:HALF] = table_times_transposed(even_ref, low + high)
+    copies[2].wait()
     out_ref[HALF:] = table_times_transposed(odd_ref, low - high)
 
 
-def pivots_kernel(place_ref, screening_ref, wave_k_ref, wave_l_ref, pivot_ref, up_ref, down_ref, far_ref, close_ref, state_ref):
+def pivots_kernel(place_ref, screening_ref, wave_k_ref, wave_l_ref, pivot_ref, up_ref, down_ref, far_ref, close_ref, chunk_ref, state_ref):
     chunk, group = place_ref[0], place_ref[1]
+    chunk_ref[...] = jnp.zeros((LINES, NY), jnp.int32) + chunk
     line = lax.broadcasted_iota(jnp.int32, (LINES, NY), 0)
     lam = jnp.zeros((LINES, NY), F32) + wave_l_ref[...]
     for k in range(LINES):
@@ -170,8 +172,7 @@
     return lax.broadcasted_iota(jnp.int32, shape, len(shape) - 1) < 64
 
 
-def forward_y_kernel(place_ref, rows_ref, even_ref, odd_t_ref, up_ref, down_ref, modes_ref, send_ref):
-    chunk = place_ref[0]
+def forward_y_kernel(chunk_ref, rows_ref, even_ref, odd_t_ref, up_ref, down_ref, modes_ref, send_ref):
     blocks = rows_ref[...].reshape(8, 8, LINES, 128)
     keep = lower_half((8, LINES, 128))
 
@@ -195,12 +196,13 @@
         plane = modes_ref[row(t)]
         upward = upward + up_ref[t] * plane
         downward = downward + down_ref[t] * plane
+    chunk = chunk_ref[...]
     for other in range(CHUNKS):
         send_ref[place_of_run(other)] = jnp.where(other > chunk, upward, downward)
 
 
-def solve_kernel(place_ref, modes_ref, arrived_ref, pivot_ref, far_ref, close_ref, even_ref, odd_ref, out_ref, solved_ref):
-    chunk = place_ref[0]
+def solve_kernel(chunk_ref, modes_ref, arrived_ref, pivot_ref, far_ref, close_ref, even_ref, odd_ref, out_ref, solved_ref):
+    chunk = chunk_ref[...]
     below = jnp.zeros((LINES, NY), F32)
     above = jnp.zeros((LINES, NY), F32)
     for other in range(CHUNKS):
@@ -295,27 +297,28 @@
     )(source, even, odd)
     columns = exchange_peers(along_x)
     planes = shape(RUN, LINES, NY)
-    pivots, up, down, far, close = call(
+    whole = jax.ShapeDtypeStruct((LINES, NY), jnp.int32)
+    pivots, up, down, far, close, chunk = call(
         pivots_kernel,
         [SMEM, SMEM, SMEM, VMEM],
-        (planes, planes, planes, shape(CHUNKS, LINES, NY), shape(LINES, NY)),
+        (planes, planes, planes, shape(CHUNKS, LINES, NY), shape(LINES, NY), whole),
         [pltpu.VMEM((2, LINES, NY), F32)],
         name="pivots",
     )(place, screening, jnp.asarray(waves), jnp.asarray(waves)[None, :])
     modes, send = call(
         forward_y_kernel,
-        [SMEM] + [VMEM] * 5,
+        [VMEM] * 6,
         (planes, shape(CHUNKS, LINES, NY)),
         name="forward_y",
-    )(place, columns, even, odd_t, up, down)
+    )(chunk, columns, even, odd_t, up, down)
     arrived = lax.all_to_all(send, "gz", 0, 0, tiled=True, axis_index_groups=RUNS)
     back_y = call(
         solve_kernel,
-        [SMEM] + [VMEM] * 7,
+        [VMEM] * 8,
         shape(8, 8, LINES, 128),
         [pltpu.VMEM((RUN, LINES, NY), F32)],
         name="solve",
-    )(place, modes, arrived, pivots, far, close, even, odd)
+    )(chunk, modes, arrived, pivots, far, close, even, odd)
     rows = exchange_peers(back_y)
     return call(backward_x_kernel, [VMEM] * 3, shape(2, 64, NX), name="backward_x")(
         rows, even, odd

time: 61.6 us -> 60.7 us (0.985)
  Pallas kernels: 6.67 us -> 5.79 us
    pallas_call x2, Pallas kernels: 1.9 us -> 0.81 us  [the longest x1 0.45 us: local(): call(solve_kernel, [VMEM] * 8, shape(8, 8, LINES, 128), [pltpu.VMEM((RUN,...]
where the time goes in v3:
time: 60.7 us; the launch traced here: 60.4 us
  blocking collectives  32.9 us (54%)
  starting transfers between devices  14.5 us (24%)
  waiting for transfers between devices  6.41 us (11%)
  Pallas kernels  5.79 us (10%)
  local copies, waits for them, and re-layouts  0.62 us (1%)
    all_to_all x1, blocking collectives, exchange_peers(): lax.all_to_all(pieces, ('gz', 'gy'), 0, 0, tiled=True, axis_index_groups=...  19.1 us
    all_to_all x1, starting transfers between devices, exchange_peers(): lax.all_to_all(pieces, ('gz', 'gy'), 0, 0, tiled=True, axis_index_groups=...  14.5 us
    all_to_all x1, blocking collectives, local(): lax.all_to_all(send, 'gz', 0, 0, tiled=True, axis_index_groups=RUNS)  13.8 us
    all_to_all x1, waiting for transfers between devices, exchange_peers(): lax.all_to_all(pieces, ('gz', 'gy'), 0, 0, tiled=True, axis_index_groups=...  6.41 us
    pallas_call x1, Pallas kernels, local(): call(forward_x_kernel, [HBM] * 3, shape(512, 128), [pltpu.VMEM((2, 64, NX...  2.39 us
    pallas_call x1, Pallas kernels, local(): call(pivots_kernel, [SMEM, SMEM, SMEM, VMEM], (planes, planes, planes, sh...  1.55 us
  transfers between devices with their start and end apart: 1, of which 1 were waited for; matrix products, arithmetic and copies ran while one was open for 0% of the time, Pallas kernels for 3%

profile of v3, /device:TPU:1, one launch (start us, length us, event | category | flops | bytes accessed | tf_op | source)
XLA Modules:
  0.0 60.4 jit_solution(10321197657827446249)
XLA Ops:
  0.0 2.4 %forward_x.1 = f32[512,128]{1,0:T(8,128)} custom-call(f32[2,64,512]{2,1,0:T(8,128)} %source_hbm.1, bf16[512,256]{1,0:T(8,128)(2,1)} %constant.47.clone.even_hbm.even_ref, bf16[512,256]{1,0:T(8,128)(2,1)} %constant.48.clone.odd_hbm.odd_ref), custom_call_target="tpu_custom_call" | custom-call | tf_op jit(solution)/shard_map/forward_x/pallas_call | solution.py:285
  2.4 0.0 copy-start
  2.4 0.0 copy-start.2
  2.4 14.5 %all-to-all-start = ((f32[64,8,128]{2,1,0:T(8,128)}), f32[64,8,128]{2,1,0:T(8,128)S(1)}, u32[]{:S(2)}, u32[]{:S(2)}) async-start(f32[64,8,128]{2,1,0:T(8,128)} %bitcast.9), calls=%async_computation | async-start | bytes 524288 | tf_op jit(solution)/shard_map/all_to_all | solution.py:273
  17.0 0.0 copy-start.4
  17.0 0.0 copy-start.3
  17.0 0.0 copy-start.5
  17.0 0.1 pad_add_fusion.place_ref
  17.1 0.6 copy-done.4
  17.7 0.0 copy-done.3
  17.7 0.0 copy-done.5
  17.7 1.6 %pivots.1 = (f32[16,8,512]{2,1,0:T(8,128)S(1)}, f32[16,8,512]{2,1,0:T(8,128)S(1)}, f32[16,8,512]{2,1,0:T(8,128)S(1)}, f32[8,8,512]{2,1,0:T(8,128)S(1)}, f32[8,512]{1,0:T(8,128)S(1)}, /*index=5*/s32[8,512]{1,0:T(8,128)S(1)}) custom-call(s32[2]{0:T(128)S(1)} %pad_add_fusion.place_ref, f32[128]{0:T(128)S(1)} %copy-done.5, f32[512]{0:T(512)S(1)} %copy-done.4, ...), custom_call_target="tpu_custom_call" | custom-call | tf_op jit(solution)/shard_map/pivots/pallas_call | solution.py:301
  19.2 6.4 %all-to-all-done = f32[64,8,128]{2,1,0:T(8,128)S(1)} async-done(((f32[64,8,128]{2,1,0:T(8,128)}), f32[64,8,128]{2,1,0:T(8,128)S(1)}, u32[]{:S(2)}, u32[]{:S(2)}) %all-to-all-start) | async-done | bytes 262176 | tf_op jit(solution)/shard_map/all_to_all | solution.py:273
  25.7 0.0 copy-done
  25.7 0.0 copy-done.2
  25.7 0.4 forward_y.1
  26.0 0.0 copy-start.1
  26.0 13.8 %all_to_all.15.arrived_ref = f32[8,8,512]{2,1,0:T(8,128)S(1)} all-to-all(f32[8,8,512]{2,1,0:T(8,128)S(1)} %get-tuple-element.17), channel_id=1, replica_groups={{256,320,384,448,0,64,128,192},{264,328,392,456,8,72,136,200},{272,336,..., dimensions={0} | all-to-all | bytes 262144 | tf_op jit(solution)/shard_map/all_to_all | solution.py:314
  39.9 0.0 copy-done.1
  39.9 0.5 solve.1
  40.3 19.1 %all_to_all.16 = f32[64,8,128]{2,1,0:T(8,128)S(1)} all-to-all(f32[64,8,128]{2,1,0:T(8,128)S(1)} %bitcast.6), channel_id=1, replica_groups={{32,33,34,35,36,37,38,39,40,41,42,43,44,45,46,47,48,49,50,51,52,53,54,5..., dimensions={0} | all-to-all | bytes 524288 | tf_op jit(solution)/shard_map/all_to_all | solution.py:273
  59.4 1.0 %backward_x.1 = f32[2,64,512]{2,1,0:T(8,128)} custom-call(f32[512,128]{1,0:T(8,128)S(1)} %bitcast.8, bf16[512,256]{1,0:T(8,128)(2,1)S(1)} %copy-done, bf16[512,256]{1,0:T(8,128)(2,1)S(1)} %copy-done.1), custom_call_target="tpu_custom_call" | custom-call | tf_op jit(solution)/shard_map/backward_x/pallas_call | solution.py:323
Async XLA Ops:
  2.4 23.3 %copy-start = (bf16[512,256]{1,0:T(8,128)(2,1)S(1)}, bf16[512,256]{1,0:T(8,128)(2,1)}, u32[]{:S(2)}) copy-start(bf16[512,256]{1,0:T(8,128)(2,1)} %constant.47.clone.even_hbm.even_ref) | copy-start | bytes 786436
  2.4 23.3 %copy-start.2 = (bf16[512,256]{1,0:T(8,128)(2,1)S(1)}, bf16[512,256]{1,0:T(8,128)(2,1)}, u32[]{:S(2)}) copy-start(bf16[512,256]{1,0:T(8,128)(2,1)} %constant.49.clone.odd_t_ref) | copy-start | bytes 786436
  2.4 23.2 %all-to-all-start = ((f32[64,8,128]{2,1,0:T(8,128)}), f32[64,8,128]{2,1,0:T(8,128)S(1)}, u32[]{:S(2)}, u32[]{:S(2)}) async-start(f32[64,8,128]{2,1,0:T(8,128)} %bitcast.9), calls=%async_computation | async-start | bytes 524288 | tf_op jit(solution)/shard_map/all_to_all | solution.py:273
  17.0 0.7 %copy-start.4 = (f32[512]{0:T(512)S(1)}, f32[512]{0:T(512)}, u32[]{:S(2)}) copy-start(f32[512]{0:T(512)} %constant.50.clone.wave_k_ref) | copy-start | bytes 6148
  17.0 0.7 %copy-start.3 = (f32[1,512]{1,0:T(1,128)S(1)}, f32[1,512]{1,0:T(1,128)}, u32[]{:S(2)}) copy-start(f32[1,512]{1,0:T(1,128)} %constant.52.wave_l_ref) | copy-start | bytes 6148
  17.0 0.7 %copy-start.5 = (f32[128]{0:T(128)S(1)}, f32[128]{0:T(128)}, u32[]{:S(2)}) copy-start(f32[128]{0:T(128)} %screening_ref.1) | copy-start | bytes 1540
  26.0 13.8 %copy-start.1 = (bf16[512,256]{1,0:T(8,128)(2,1)S(1)}, bf16[512,256]{1,0:T(8,128)(2,1)}, u32[]{:S(2)}) copy-start(bf16[512,256]{1,0:T(8,128)(2,1)} %constant.48.clone.odd_hbm.odd_ref) | copy-start | bytes 786436

commit v4 on v3

--- a/solution.py
+++ b/solution.py
@@ -17,8 +17,11 @@
 RUN = NZ // CHUNKS
 LINES = 8
 PEERS = 64
-FIRST_RUN = 4
-FIRST_Y = 4
+RUN_ORDER = (4, 3, 5, 2, 6, 1, 7, 0)
+Y_IN = (4, 5, 6, 7, 0, 1, 2, 3)
+G_IN = (7, 0, 1, 2, 3, 4, 5, 6)
+Y_OUT = (4, 5, 6, 7, 0, 1, 2, 3)
+G_OUT = (5, 4, 7, 6, 1, 0, 3, 2)
 
 F32 = jnp.float32
 BF16 = jnp.bfloat16
@@ -72,12 +75,8 @@
     return product[:HALF, :rows] + (product[:HALF, rows:] + product[HALF:, :rows])
 
 
-def row(plane):
-    return (plane - 2 * FIRST_Y) % RUN
-
-
-def place_of_run(run):
-    return (run - FIRST_RUN) % CHUNKS
+def row(plane, order):
+    return 2 * order.index(plane // 2) + plane % 2
 
 
 def forward_x_kernel(source_hbm, even_hbm, odd_hbm, out_ref, source_ref, even_ref, odd_ref, arrived):
@@ -88,12 +87,11 @@
     ]
     for copy in copies:
         copy.start()
-    copies[0].wait()
+    for copy in copies:
+        copy.wait()
     rows = source_ref[...].reshape(128, NX)
     low, high = rows[:, :HALF], rows[:, HALF:]
-    copies[1].wait()
     out_ref[:HALF] = table_times_transposed(even_ref, low + high)
-    copies[2].wait()
     out_ref[HALF:] = table_times_transposed(odd_ref, low - high)
 
 
@@ -176,6 +174,9 @@
     blocks = rows_ref[...].reshape(8, 8, LINES, 128)
     keep = lower_half((8, LINES, 128))
 
+    def at(g):
+        return blocks[:, G_IN.index(g)]
+
     def gather(parts):
         columns = []
         for pair in range(2):
@@ -185,20 +186,20 @@
             columns.append(jnp.stack([first, second], axis=1).reshape(128, 128))
         return jnp.concatenate(columns, axis=1)
 
-    sums = gather([blocks[:, g] + blocks[:, g + 4] for g in range(4)])
-    differences = gather([blocks[:, g] - blocks[:, g + 4] for g in range(4)])
+    sums = gather([at(g) + at(g + 4) for g in range(4)])
+    differences = gather([at(g) - at(g + 4) for g in range(4)])
     modes_ref[:, :, :HALF] = times_table(sums, even_ref).reshape(RUN, LINES, HALF)
     modes_ref[:, :, HALF:] = times_table(differences, odd_t_ref).reshape(RUN, LINES, HALF)
 
     upward = jnp.zeros((LINES, NY), F32)
     downward = jnp.zeros((LINES, NY), F32)
     for t in range(RUN):
-        plane = modes_ref[row(t)]
+        plane = modes_ref[row(t, Y_IN)]
         upward = upward + up_ref[t] * plane
         downward = downward + down_ref[t] * plane
     chunk = chunk_ref[...]
     for other in range(CHUNKS):
-        send_ref[place_of_run(other)] = jnp.where(other > chunk, upward, downward)
+        send_ref[RUN_ORDER.index(other)] = jnp.where(other > chunk, upward, downward)
 
 
 def solve_kernel(chunk_ref, modes_ref, arrived_ref, pivot_ref, far_ref, close_ref, even_ref, odd_ref, out_ref, solved_ref):
@@ -206,19 +207,19 @@
     below = jnp.zeros((LINES, NY), F32)
     above = jnp.zeros((LINES, NY), F32)
     for other in range(CHUNKS):
-        below = jnp.where(other < chunk, arrived_ref[place_of_run(other)] + far_ref[other] * below, below)
+        below = jnp.where(other < chunk, arrived_ref[RUN_ORDER.index(other)] + far_ref[other] * below, below)
         rest = CHUNKS - 1 - other
-        above = jnp.where(rest > chunk, arrived_ref[place_of_run(rest)] + far_ref[rest] * above, above)
+        above = jnp.where(rest > chunk, arrived_ref[RUN_ORDER.index(rest)] + far_ref[rest] * above, above)
 
     elimination = below
     for t in range(RUN):
-        elimination = pivot_ref[t] * (modes_ref[row(t)] + elimination)
-        solved_ref[row(t)] = elimination
+        elimination = pivot_ref[t] * (modes_ref[row(t, Y_IN)] + elimination)
+        solved_ref[row(t, Y_OUT)] = elimination
     value = (elimination + pivot_ref[RUN - 1] * above) * close_ref[...]
-    solved_ref[row(RUN - 1)] = value
+    solved_ref[row(RUN - 1, Y_OUT)] = value
     for t in reversed(range(RUN - 1)):
-        value = solved_ref[row(t)] + pivot_ref[t] * value
-        solved_ref[row(t)] = value
+        value = solved_ref[row(t, Y_OUT)] + pivot_ref[t] * value
+        solved_ref[row(t, Y_OUT)] = value
 
     solved = solved_ref[...].reshape(128, NY)
     even = times_table(solved[:, :HALF], even_ref)
@@ -228,12 +229,14 @@
         for pair in range(2):
             column = values[:, pair * 128 : pair * 128 + 128].reshape(8, 2, LINES, 128)
             a, b = column[:, 0], column[:, 1]
-            out_ref[:, base + 2 * pair] = jnp.where(keep, a, swap_halves(b))
-            out_ref[:, base + 2 * pair + 1] = jnp.where(keep, swap_halves(a), b)
+            out_ref[:, G_OUT.index(base + 2 * pair)] = jnp.where(keep, a, swap_halves(b))
+            out_ref[:, G_OUT.index(base + 2 * pair + 1)] = jnp.where(keep, swap_halves(a), b)
 
 
 def backward_x_kernel(rows_ref, even_ref, odd_ref, out_ref):
-    values = rows_ref[...].T
+    blocks = rows_ref[...].reshape(8, 8, LINES, 128)
+    ordered = [blocks[Y_OUT.index(y), G_OUT.index(g)] for y in Y_IN for g in G_IN]
+    values = jnp.concatenate(ordered, axis=0).T
     even = times_table(values[:, :HALF], even_ref)
     odd = times_table(values[:, HALF:], odd_ref)
     scale = 1.0 / (NX * NY)
@@ -262,16 +265,17 @@
     return jax.ShapeDtypeStruct(sizes, F32)
 
 
-RUN_PEERS = [
-    [run * PEERS + (peer + FIRST_Y * 8) % PEERS for peer in range(PEERS)] for run in range(CHUNKS)
-]
-RUNS = [[(run + FIRST_RUN) % CHUNKS * 8 + y for run in range(CHUNKS)] for y in range(8)]
-
-
-def exchange_peers(values):
+def run_peers(along_y, along_g):
+    return [[run * PEERS + y * 8 + g for y in along_y for g in along_g] for run in range(CHUNKS)]
+
+
+RUNS = [[run * 8 + y for run in RUN_ORDER] for y in range(8)]
+
+
+def exchange_peers(values, along_y, along_g):
     pieces = values.reshape(PEERS, LINES, 128)
     pieces = lax.all_to_all(
-        pieces, ("gz", "gy"), 0, 0, tiled=True, axis_index_groups=RUN_PEERS
+        pieces, ("gz", "gy"), 0, 0, tiled=True, axis_index_groups=run_peers(along_y, along_g)
     )
     return pieces.reshape(512, 128)
 
@@ -280,7 +284,9 @@
     even, odd, odd_t = (jnp.asarray(table) for table in half_tables())
     waves = wave_terms()
     gz, gy = lax.axis_index("gz"), lax.axis_index("gy")
-    place = jnp.stack([gz // 8, (gz + 8 - FIRST_Y) % 8 * 8 + gy]).astype(jnp.int32)
+    place_y = jnp.asarray([Y_IN.index(y) for y in range(8)], jnp.int32)[gz % 8]
+    place_g = jnp.asarray([G_IN.index(g) for g in range(8)], jnp.int32)[gy]
+    place = jnp.stack([gz // 8, place_y * 8 + place_g]).astype(jnp.int32)
 
     along_x = call(
         forward_x_kernel,
@@ -295,7 +301,7 @@
         name="forward_x",
         limit=60 * 1024 * 1024,
     )(source, even, odd)
-    columns = exchange_peers(along_x)
+    columns = exchange_peers(along_x, Y_IN, G_IN)
     planes = shape(RUN, LINES, NY)
     whole = jax.ShapeDtypeStruct((LINES, NY), jnp.int32)
     pivots, up, down, far, close, chunk = call(
@@ -319,7 +325,7 @@
         [pltpu.VMEM((RUN, LINES, NY), F32)],
         name="solve",
     )(chunk, modes, arrived, pivots, far, close, even, odd)
-    rows = exchange_peers(back_y)
+    rows = exchange_peers(back_y, Y_OUT, G_OUT)
     return call(backward_x_kernel, [VMEM] * 3, shape(2, 64, NX), name="backward_x")(
         rows, even, odd
     )

time: 60.7 us -> 58.9 us (0.970)
  waiting for transfers between devices: 6.41 us -> 1.83 us
  blocking collectives: 32.9 us -> 30.9 us
  starting transfers between devices: 14.5 us -> 16.4 us
  local copies, waits for them, and re-layouts: 0.62 us -> 2.51 us
  between operations: 0.12 us -> 1.35 us
    all_to_all x1, waiting for transfers between devices: 6.41 us -> 1.83 us  [exchange_peers(): lax.all_to_all(pieces, ('gz', 'gy'), 0, 0, tiled=True, axis_index_groups=...]
    all_to_all x1, starting transfers between devices: 14.5 us -> 16.4 us  [exchange_peers(): lax.all_to_all(pieces, ('gz', 'gy'), 0, 0, tiled=True, axis_index_groups=...]
    dynamic_slice x0 -> x2, local copies, waits for them, and re-layouts: none -> 1.19 us  [the longest x1 0.61 us: local(): place_g = jnp.asarray([G_IN.index(g) for g in range(8)], jnp.int32)[gy]]
    all_to_all x1, blocking collectives: 13.8 us -> 12.7 us  [local(): lax.all_to_all(send, 'gz', 0, 0, tiled=True, axis_index_groups=RUNS)]
    all_to_all x1, blocking collectives: 19.1 us -> 18.2 us  [exchange_peers(): lax.all_to_all(pieces, ('gz', 'gy'), 0, 0, tiled=True, axis_index_groups=...]
    unnamed x12 -> x16, local copies, waits for them, and re-layouts: 0.62 us -> 1.32 us
  transfers between devices with their start and end apart: 1 -> 1, of which waited for: 1 -> 1; matrix products, arithmetic and copies ran while one was open for 0% -> 2% of each run, Pallas kernels for 3% -> 3%
where the time goes in v4:
time: 58.9 us; the launch traced here: 58.5 us
  blocking collectives  30.9 us (52%)
  starting transfers between devices  16.4 us (28%)
  Pallas kernels  5.57 us (9%)
  local copies, waits for them, and re-layouts  2.51 us (4%)
  waiting for transfers between devices  1.83 us (3%)
  between operations  1.35 us (2%)
    all_to_all x1, blocking collectives, exchange_peers(): lax.all_to_all(pieces, ('gz', 'gy'), 0, 0, tiled=True, axis_index_groups=...  18.2 us
    all_to_all x1, starting transfers between devices, exchange_peers(): lax.all_to_all(pieces, ('gz', 'gy'), 0, 0, tiled=True, axis_index_groups=...  16.4 us
    all_to_all x1, blocking collectives, local(): lax.all_to_all(send, 'gz', 0, 0, tiled=True, axis_index_groups=RUNS)  12.7 us
    pallas_call x1, Pallas kernels, local(): call(forward_x_kernel, [HBM] * 3, shape(512, 128), [pltpu.VMEM((2, 64, NX...  2.17 us
    all_to_all x1, waiting for transfers between devices, exchange_peers(): lax.all_to_all(pieces, ('gz', 'gy'), 0, 0, tiled=True, axis_index_groups=...  1.83 us
    pallas_call x1, Pallas kernels, local(): call(pivots_kernel, [SMEM, SMEM, SMEM, VMEM], (planes, planes, planes, sh...  1.55 us
    unnamed x16, local copies, waits for them, and re-layouts  1.32 us
  transfers between devices with their start and end apart: 1, of which 1 were waited for; matrix products, arithmetic and copies ran while one was open for 2% of the time, Pallas kernels for 3%

profile of v4, /device:TPU:1, one launch (start us, length us, event | category | flops | bytes accessed | tf_op | source)
XLA Modules:
  0.0 58.5 jit_solution(2863635404382351380)
XLA Ops:
  0.0 2.2 %forward_x.1 = f32[512,128]{1,0:T(8,128)} custom-call(f32[2,64,512]{2,1,0:T(8,128)} %source_hbm.1, bf16[512,256]{1,0:T(8,128)(2,1)} %constant.50.clone.even_hbm.even_ref, bf16[512,256]{1,0:T(8,128)(2,1)} %constant.51.clone.odd_hbm.odd_ref), custom_call_target="tpu_custom_call" | custom-call | tf_op jit(solution)/shard_map/forward_x/pallas_call | solution.py:291
  2.2 0.0 copy-start
  2.2 0.0 copy-start.2
  2.2 16.4 %all-to-all-start = ((f32[64,8,128]{2,1,0:T(8,128)}), f32[64,8,128]{2,1,0:T(8,128)S(1)}, u32[]{:S(2)}, u32[]{:S(2)}) async-start(f32[64,8,128]{2,1,0:T(8,128)} %bitcast.8), calls=%async_computation | async-start | bytes 524288 | tf_op jit(solution)/shard_map/all_to_all | solution.py:277
  18.6 0.0 copy-start.7
  18.6 0.6 %copy-done.7 = s32[8]{0:T(128)S(1)} copy-done((s32[8]{0:T(128)S(1)}, s32[8]{0:T(128)}, u32[]{:S(2)}) %copy-start.7) | copy-done | bytes 56
  19.3 0.0 copy-start.6
  19.3 0.6 %dynamic_slice.7 = s32[1]{0:T(128)} dynamic-slice(s32[8]{0:T(128)S(1)} %copy-done.7, s32[]{:T(128)S(6)} %select_n.20), dynamic_slice_sizes={1} | dynamic-slice | bytes 12 | tf_op jit(solution)/shard_map/dynamic_slice | solution.py:288
  19.9 0.0 copy-done.6
  19.9 0.6 dynamic_slice.6
  21.1 0.0 copy-start.4
  21.7 0.0 copy-start.3
  21.7 0.0 copy-start.5
  21.7 0.1 pad_add_fusion.place_ref
  21.8 0.0 copy-done.4
  21.8 0.6 copy-done.3
  22.4 0.0 copy-done.5
  22.4 1.6 %pivots.1 = (f32[16,8,512]{2,1,0:T(8,128)S(1)}, f32[16,8,512]{2,1,0:T(8,128)S(1)}, f32[16,8,512]{2,1,0:T(8,128)S(1)}, f32[8,8,512]{2,1,0:T(8,128)S(1)}, f32[8,512]{1,0:T(8,128)S(1)}, /*index=5*/s32[8,512]{1,0:T(8,128)S(1)}) custom-call(s32[2]{0:T(128)S(1)} %pad_add_fusion.place_ref, f32[128]{0:T(128)S(1)} %copy-done.5, f32[512]{0:T(512)S(1)} %copy-done.4, ...), custom_call_target="tpu_custom_call" | custom-call | tf_op jit(solution)/shard_map/pivots/pallas_call | solution.py:307
  24.0 1.8 %all-to-all-done = f32[64,8,128]{2,1,0:T(8,128)S(1)} async-done(((f32[64,8,128]{2,1,0:T(8,128)}), f32[64,8,128]{2,1,0:T(8,128)S(1)}, u32[]{:S(2)}, u32[]{:S(2)}) %all-to-all-start) | async-done | bytes 262176 | tf_op jit(solution)/shard_map/all_to_all | solution.py:277
  25.8 0.0 copy-done
  25.8 0.0 copy-done.2
  25.8 0.4 forward_y.1
  26.2 0.0 copy-start.1
  26.2 12.7 %all_to_all.15.arrived_ref = f32[8,8,512]{2,1,0:T(8,128)S(1)} all-to-all(f32[8,8,512]{2,1,0:T(8,128)S(1)} %get-tuple-element.17), channel_id=1, replica_groups={{256,192,320,128,384,64,448,0},{264,200,328,136,392,72,456,8},{272,208,..., dimensions={0} | all-to-all | bytes 262144 | tf_op jit(solution)/shard_map/all_to_all | solution.py:320
  38.8 0.0 copy-done.1
  38.8 0.5 solve.1
  39.3 18.2 %all_to_all.16 = f32[64,8,128]{2,1,0:T(8,128)S(1)} all-to-all(f32[64,8,128]{2,1,0:T(8,128)S(1)} %bitcast.5), channel_id=1, replica_groups={{37,36,39,38,33,32,35,34,45,44,47,46,41,40,43,42,53,52,55,54,49,48,51,5..., dimensions={0} | all-to-all | bytes 524288 | tf_op jit(solution)/shard_map/all_to_all | solution.py:277
  57.5 1.0 %backward_x.1 = f32[2,64,512]{2,1,0:T(8,128)} custom-call(f32[512,128]{1,0:T(8,128)S(1)} %bitcast.7, bf16[512,256]{1,0:T(8,128)(2,1)S(1)} %copy-done, bf16[512,256]{1,0:T(8,128)(2,1)S(1)} %copy-done.1), custom_call_target="tpu_custom_call" | custom-call | tf_op jit(solution)/shard_map/backward_x/pallas_call | solution.py:329
Async XLA Ops:
  2.2 23.6 %copy-start = (bf16[512,256]{1,0:T(8,128)(2,1)S(1)}, bf16[512,256]{1,0:T(8,128)(2,1)}, u32[]{:S(2)}) copy-start(bf16[512,256]{1,0:T(8,128)(2,1)} %constant.50.clone.even_hbm.even_ref) | copy-start | bytes 786436
  2.2 23.6 %copy-start.2 = (bf16[512,256]{1,0:T(8,128)(2,1)S(1)}, bf16[512,256]{1,0:T(8,128)(2,1)}, u32[]{:S(2)}) copy-start(bf16[512,256]{1,0:T(8,128)(2,1)} %constant.52.clone.odd_t_ref) | copy-start | bytes 786436
  2.2 23.6 %all-to-all-start = ((f32[64,8,128]{2,1,0:T(8,128)}), f32[64,8,128]{2,1,0:T(8,128)S(1)}, u32[]{:S(2)}, u32[]{:S(2)}) async-start(f32[64,8,128]{2,1,0:T(8,128)} %bitcast.8), calls=%async_computation | async-start | bytes 524288 | tf_op jit(solution)/shard_map/all_to_all | solution.py:277
  18.6 0.7 %copy-start.7 = (s32[8]{0:T(128)S(1)}, s32[8]{0:T(128)}, u32[]{:S(2)}) copy-start(s32[8]{0:T(128)} %constant.54.clone) | copy-start | bytes 100
  19.3 0.7 %copy-start.6 = (s32[8]{0:T(128)S(1)}, s32[8]{0:T(128)}, u32[]{:S(2)}) copy-start(s32[8]{0:T(128)} %constant.53.clone) | copy-start | bytes 100
  21.1 0.8 %copy-start.4 = (f32[512]{0:T(512)S(1)}, f32[512]{0:T(512)}, u32[]{:S(2)}) copy-start(f32[512]{0:T(512)} %constant.55.clone.wave_k_ref) | copy-start | bytes 6148
  21.7 0.7 %copy-start.3 = (f32[1,512]{1,0:T(1,128)S(1)}, f32[1,512]{1,0:T(1,128)}, u32[]{:S(2)}) copy-start(f32[1,512]{1,0:T(1,128)} %constant.57.wave_l_ref) | copy-start | bytes 6148
  21.7 0.7 %copy-start.5 = (f32[128]{0:T(128)S(1)}, f32[128]{0:T(128)}, u32[]{:S(2)}) copy-start(f32[128]{0:T(128)} %screening_ref.1) | copy-start | bytes 1540
  26.2 12.7 %copy-start.1 = (bf16[512,256]{1,0:T(8,128)(2,1)S(1)}, bf16[512,256]{1,0:T(8,128)(2,1)}, u32[]{:S(2)}) copy-start(bf16[512,256]{1,0:T(8,128)(2,1)} %constant.51.clone.odd_hbm.odd_ref) | copy-start | bytes 786436

commit v5 on v4

--- a/solution.py
+++ b/solution.py
@@ -23,6 +23,8 @@
 Y_OUT = (4, 5, 6, 7, 0, 1, 2, 3)
 G_OUT = (5, 4, 7, 6, 1, 0, 3, 2)
 
+X_KERNEL_VMEM = 55574528
+
 F32 = jnp.float32
 BF16 = jnp.bfloat16
 
@@ -47,7 +49,7 @@
 
 def wave_terms():
     index = np.concatenate([np.arange(0, 512, 2), np.arange(1, 512, 2)])
-    return (4.0 * np.sin(index * (math.pi / 512)) ** 2).astype(np.float32)
+    return (4.0 * np.sin(index * (math.pi / 512)) ** 2).astype(np.float32).reshape(4, 128)
 
 
 def split(values):
@@ -79,7 +81,68 @@
     return 2 * order.index(plane // 2) + plane % 2
 
 
-def forward_x_kernel(source_hbm, even_hbm, odd_hbm, out_ref, source_ref, even_ref, odd_ref, arrived):
+def own_place():
+    gz, gy = lax.axis_index("gz"), lax.axis_index("gy")
+    return gz >> 3, (((gz & 7) + 8 - Y_IN[0]) & 7) * 8 + ((gy + 8 - G_IN[0]) & 7)
+
+
+def pivots(screening_ref, waves_ref, shift_ref, column_ref, pivot_ref, down_ref, far_ref, close_ref, chunk_ref):
+    chunk, group = own_place()
+    chunk_ref[...] = jnp.zeros((LINES, NY), jnp.int32) + chunk
+    shift_ref[...] = jnp.broadcast_to(screening_ref[...], (NZ, NZ)).T
+    column_ref[...] = jnp.broadcast_to(waves_ref[pl.ds(group >> 4, 1), :], (128, 128)).T
+    along_k = column_ref[pl.ds(pl.multiple_of((group & 15) * LINES, LINES), LINES), :]
+    lam = jnp.concatenate([waves_ref[q : q + 1, :] + along_k for q in range(4)], axis=1)
+    one = jnp.ones((LINES, NY), F32)
+
+    def step(plane, total, rise):
+        shift = shift_ref[pl.ds(plane, 1), :]
+        rise = rise + (jnp.concatenate([shift] * 4, axis=1) + lam) * total
+        return total + rise, rise
+
+    below, above = one, one
+    own_below, own_above = one, one
+    for index in range(CHUNKS - 1):
+        other = CHUNKS - 1 - index
+        low_total, low_rise, high_total, high_rise = one, below, one, above
+        for t in range(RUN):
+            low_total, low_rise = step(index * RUN + t, low_total, low_rise)
+            high_total, high_rise = step(other * RUN + RUN - 1 - t, high_total, high_rise)
+        low_inverse, high_inverse = 1.0 / low_total, 1.0 / high_total
+
+        @pl.when(index < chunk)
+        def _():
+            far_ref[index] = low_inverse
+
+        @pl.when(other > chunk)
+        def _():
+            far_ref[other] = high_inverse
+
+        below, above = low_rise * low_inverse, high_rise * high_inverse
+        own_below = jnp.where(chunk == index + 1, below, own_below)
+        own_above = jnp.where(chunk == other - 1, above, own_above)
+    far_ref[chunk] = jnp.zeros((LINES, NY), F32)
+
+    first = chunk * RUN
+    total, rise, high_total, high_rise = one, own_below, one, own_above
+    for t in range(RUN):
+        down_ref[RUN - 1 - t] = high_total
+        before = total
+        total, rise = step(first + t, total, rise)
+        pivot_ref[t] = before / total
+        high_total, high_rise = step(first + RUN - 1 - t, high_total, high_rise)
+    inverse = 1.0 / total
+    close_ref[...] = 1.0 / (rise * inverse + pivot_ref[RUN - 1] * own_above)
+    high_inverse = 1.0 / high_total
+    for t in range(RUN):
+        down_ref[t] = down_ref[t] * high_inverse
+
+
+def forward_x_kernel(
+    screening_ref, waves_ref, source_hbm, even_hbm, odd_hbm,
+    out_ref, pivot_ref, down_ref, far_ref, close_ref, chunk_ref,
+    source_ref, even_ref, odd_ref, shift_ref, column_ref, arrived,
+):
     copies = [
         pltpu.make_async_copy(source_hbm, source_ref, arrived.at[0]),
         pltpu.make_async_copy(even_hbm, even_ref, arrived.at[1]),
@@ -87,6 +150,10 @@
     ]
     for copy in copies:
         copy.start()
+    pivots(
+        screening_ref, waves_ref, shift_ref, column_ref,
+        pivot_ref, down_ref, far_ref, close_ref, chunk_ref,
+    )
     for copy in copies:
         copy.wait()
     rows = source_ref[...].reshape(128, NX)
@@ -95,72 +162,6 @@
     out_ref[HALF:] = table_times_transposed(odd_ref, low - high)
 
 
-def pivots_kernel(place_ref, screening_ref, wave_k_ref, wave_l_ref, pivot_ref, up_ref, down_ref, far_ref, close_ref, chunk_ref, state_ref):
-    chunk, group = place_ref[0], place_ref[1]
-    chunk_ref[...] = jnp.zeros((LINES, NY), jnp.int32) + chunk
-    line = lax.broadcasted_iota(jnp.int32, (LINES, NY), 0)
-    lam = jnp.zeros((LINES, NY), F32) + wave_l_ref[...]
-    for k in range(LINES):
-        lam = lam + jnp.where(line == k, wave_k_ref[group * LINES + k], 0.0)
-    one = jnp.ones((LINES, NY), F32)
-
-    def step(plane, total, rise):
-        rise = rise + (screening_ref[plane] + lam) * total
-        return total + rise, rise
-
-    def lap(index, state):
-        below, above = state
-        other = CHUNKS - 1 - index
-
-        @pl.when(index == chunk)
-        def _():
-            state_ref[0] = below
-
-        @pl.when(other == chunk)
-        def _():
-            state_ref[1] = above
-
-        low_total, low_rise, high_total, high_rise = one, below, one, above
-        for t in range(RUN):
-            low_total, low_rise = step(index * RUN + t, low_total, low_rise)
-            high_total, high_rise = step(other * RUN + RUN - 1 - t, high_total, high_rise)
-        low_inverse, high_inverse = 1.0 / low_total, 1.0 / high_total
-
-        @pl.when(index < chunk)
-        def _():
-            far_ref[index] = low_inverse
-
-        @pl.when(other > chunk)
-        def _():
-            far_ref[other] = high_inverse
-
-        return low_rise * low_inverse, high_rise * high_inverse
-
-    far_ref[chunk] = jnp.zeros((LINES, NY), F32)
-    lax.fori_loop(0, CHUNKS, lap, (one, one))
-
-    first = chunk * RUN
-    total, rise = one, state_ref[0]
-    for t in range(RUN):
-        up_ref[t] = total
-        before = total
-        total, rise = step(first + t, total, rise)
-        pivot_ref[t] = before / total
-    inverse = 1.0 / total
-    last_pivot = pivot_ref[RUN - 1]
-    close_ref[...] = 1.0 / (rise * inverse + last_pivot * state_ref[1])
-    for t in range(RUN):
-        up_ref[t] = up_ref[t] * inverse
-
-    total, rise = one, state_ref[1]
-    for t in reversed(range(RUN)):
-        down_ref[t] = total
-        total, rise = step(first + t, total, rise)
-    inverse = 1.0 / total
-    for t in range(RUN):
-        down_ref[t] = down_ref[t] * inverse
-
-
 def swap_halves(values):
     shape = values.shape
     return pltpu.roll(values.reshape(-1, 128), 64, 1).reshape(shape)
@@ -170,7 +171,7 @@
     return lax.broadcasted_iota(jnp.int32, shape, len(shape) - 1) < 64
 
 
-def forward_y_kernel(chunk_ref, rows_ref, even_ref, odd_t_ref, up_ref, down_ref, modes_ref, send_ref):
+def forward_y_kernel(chunk_ref, rows_ref, even_ref, odd_t_ref, pivot_ref, down_ref, modes_ref, send_ref):
     blocks = rows_ref[...].reshape(8, 8, LINES, 128)
     keep = lower_half((8, LINES, 128))
 
@@ -195,7 +196,7 @@
     downward = jnp.zeros((LINES, NY), F32)
     for t in range(RUN):
         plane = modes_ref[row(t, Y_IN)]
-        upward = upward + up_ref[t] * plane
+        upward = pivot_ref[t] * (plane + upward)
         downward = downward + down_ref[t] * plane
     chunk = chunk_ref[...]
     for other in range(CHUNKS):
@@ -283,40 +284,30 @@
 def local(source, screening):
     even, odd, odd_t = (jnp.asarray(table) for table in half_tables())
     waves = wave_terms()
-    gz, gy = lax.axis_index("gz"), lax.axis_index("gy")
-    place_y = jnp.asarray([Y_IN.index(y) for y in range(8)], jnp.int32)[gz % 8]
-    place_g = jnp.asarray([G_IN.index(g) for g in range(8)], jnp.int32)[gy]
-    place = jnp.stack([gz // 8, place_y * 8 + place_g]).astype(jnp.int32)
-
-    along_x = call(
+    planes = shape(RUN, LINES, NY)
+    whole = jax.ShapeDtypeStruct((LINES, NY), jnp.int32)
+    along_x, pivot, down, far, close, chunk = call(
         forward_x_kernel,
-        [HBM] * 3,
-        shape(512, 128),
+        [VMEM] * 2 + [HBM] * 3,
+        (shape(512, 128), planes, planes, shape(CHUNKS, LINES, NY), shape(LINES, NY), whole),
         [
             pltpu.VMEM((2, 64, NX), F32),
             pltpu.VMEM((2 * HALF, HALF), BF16),
             pltpu.VMEM((2 * HALF, HALF), BF16),
+            pltpu.VMEM((NZ, NZ), F32),
+            pltpu.VMEM((128, 128), F32),
             pltpu.SemaphoreType.DMA((3,)),
         ],
         name="forward_x",
-        limit=60 * 1024 * 1024,
-    )(source, even, odd)
+        limit=X_KERNEL_VMEM,
+    )(screening[None, :], jnp.asarray(waves), source, even, odd)
     columns = exchange_peers(along_x, Y_IN, G_IN)
-    planes = shape(RUN, LINES, NY)
-    whole = jax.ShapeDtypeStruct((LINES, NY), jnp.int32)
-    pivots, up, down, far, close, chunk = call(
-        pivots_kernel,
-        [SMEM, SMEM, SMEM, VMEM],
-        (planes, planes, planes, shape(CHUNKS, LINES, NY), shape(LINES, NY), whole),
-        [pltpu.VMEM((2, LINES, NY), F32)],
-        name="pivots",
-    )(place, screening, jnp.asarray(waves), jnp.asarray(waves)[None, :])
     modes, send = call(
         forward_y_kernel,
         [VMEM] * 6,
         (planes, shape(CHUNKS, LINES, NY)),
         name="forward_y",
-    )(chunk, columns, even, odd_t, up, down)
+    )(chunk, columns, even, odd_t, pivot, down)
     arrived = lax.all_to_all(send, "gz", 0, 0, tiled=True, axis_index_groups=RUNS)
     back_y = call(
         solve_kernel,
@@ -324,7 +315,7 @@
         shape(8, 8, LINES, 128),
         [pltpu.VMEM((RUN, LINES, NY), F32)],
         name="solve",
-    )(chunk, modes, arrived, pivots, far, close, even, odd)
+    )(chunk, modes, arrived, pivot, far, close, even, odd)
     rows = exchange_peers(back_y, Y_OUT, G_OUT)
     return call(backward_x_kernel, [VMEM] * 3, shape(2, 64, NX), name="backward_x")(
         rows, even, odd

time: 58.9 us -> 58.3 us (0.990)
  blocking collectives: 30.9 us -> 53.9 us
  starting transfers between devices: 16.4 us -> 0 us
  Pallas kernels: 5.57 us -> 3.35 us
  waiting for transfers between devices: 1.83 us -> 0 us
  local copies, waits for them, and re-layouts: 2.51 us -> 0.7 us
  between operations: 1.35 us -> 0.05 us
    all_to_all x1 -> x2, blocking collectives: 18.2 us -> 41.6 us  [exchange_peers(): lax.all_to_all(pieces, ('gz', 'gy'), 0, 0, tiled=True, axis_index_groups=...]
    all_to_all x1 -> x0, starting transfers between devices: 16.4 us -> none  [exchange_peers(): lax.all_to_all(pieces, ('gz', 'gy'), 0, 0, tiled=True, axis_index_groups=...]
    pallas_call x2 -> x1, Pallas kernels: 3.73 us -> 1.49 us  [local(): call(forward_x_kernel, [VMEM] * 2 + [HBM] * 3, (shape(512, 128), planes,...]
    all_to_all x1 -> x0, waiting for transfers between devices: 1.83 us -> none  [exchange_peers(): lax.all_to_all(pieces, ('gz', 'gy'), 0, 0, tiled=True, axis_index_groups=...]
    dynamic_slice x2 -> x0, local copies, waits for them, and re-layouts: 1.19 us -> none  [the longest x1 0.61 us: local(): place_g = jnp.asarray([G_IN.index(g) for g in range(8)], jnp.int32)[gy]]
    unnamed x16 -> x10, local copies, waits for them, and re-layouts: 1.32 us -> 0.7 us
  transfers between devices with their start and end apart: 1 -> 0, of which waited for: 1 -> 0; matrix products, arithmetic and copies ran while one was open for 2% -> 0% of each run, Pallas kernels for 3% -> 0%
where the time goes in v5:
time: 58.3 us; the launch traced here: 58 us
  blocking collectives  53.9 us (92%)
  Pallas kernels  3.35 us (6%)
  local copies, waits for them, and re-layouts  0.7 us (1%)
    all_to_all x2, blocking collectives, exchange_peers(): lax.all_to_all(pieces, ('gz', 'gy'), 0, 0, tiled=True, axis_index_groups=...  41.6 us
    all_to_all x1, blocking collectives, local(): lax.all_to_all(send, 'gz', 0, 0, tiled=True, axis_index_groups=RUNS)  12.3 us
    pallas_call x1, Pallas kernels, local(): call(forward_x_kernel, [VMEM] * 2 + [HBM] * 3, (shape(512, 128), planes,...  1.49 us

profile of v5, /device:TPU:1, one launch (start us, length us, event | category | flops | bytes accessed | tf_op | source)
XLA Modules:
  0.0 58.0 jit_solution(5866295597572417045)
XLA Ops:
  0.0 0.0 copy-start.3
  0.0 0.0 copy-start.4
  0.0 0.7 %copy-done.3 = f32[4,128]{1,0:T(4,128)S(1)} copy-done((f32[4,128]{1,0:T(4,128)S(1)}, f32[4,128]{1,0:T(4,128)}, u32[]{:S(2)}) %copy-start.3) | copy-done | bytes 2072
  0.7 0.0 copy-done.4
  0.7 1.5 %forward_x.1 = (f32[512,128]{1,0:T(8,128)S(1)}, f32[16,8,512]{2,1,0:T(8,128)S(1)}, f32[16,8,512]{2,1,0:T(8,128)S(1)}, f32[8,8,512]{2,1,0:T(8,128)S(1)}, f32[8,512]{1,0:T(8,128)S(1)}, /*index=5*/s32[8,512]{1,0:T(8,128)S(1)}) custom-call(f32[1,128]{1,0:T(1,128)S(1)} %bitcast.9, f32[4,128]{1,0:T(4,128)S(1)} %copy-done.3, f32[2,64,512]{2,1,0:T(8,128)} %source_hbm.1, ...), custom_call_target="tpu_custom_call" | custom-call | tf_op jit(solution)/shard_map/forward_x/pallas_call | solution.py:289
  2.2 0.0 copy-start
  2.2 0.0 copy-start.2
  2.2 23.4 %all_to_all.15 = f32[64,8,128]{2,1,0:T(8,128)S(1)} all-to-all(f32[64,8,128]{2,1,0:T(8,128)S(1)} %bitcast.8), channel_id=1, replica_groups={{39,32,33,34,35,36,37,38,47,40,41,42,43,44,45,46,55,48,49,50,51,52,53,5..., dimensions={0} | all-to-all | bytes 524288 | tf_op jit(solution)/shard_map/all_to_all | solution.py:278
  25.6 0.0 copy-done
  25.6 0.0 copy-done.2
  25.6 0.4 forward_y.1
  26.0 0.0 copy-start.1
  26.0 12.3 %all_to_all.16.arrived_ref = f32[8,8,512]{2,1,0:T(8,128)S(1)} all-to-all(f32[8,8,512]{2,1,0:T(8,128)S(1)} %get-tuple-element.18), channel_id=1, replica_groups={{256,192,320,128,384,64,448,0},{264,200,328,136,392,72,456,8},{272,208,..., dimensions={0} | all-to-all | bytes 262144 | tf_op jit(solution)/shard_map/all_to_all | solution.py:311
  38.3 0.0 copy-done.1
  38.3 0.5 solve.1
  38.8 18.2 %all_to_all.17 = f32[64,8,128]{2,1,0:T(8,128)S(1)} all-to-all(f32[64,8,128]{2,1,0:T(8,128)S(1)} %bitcast.5), channel_id=1, replica_groups={{37,36,39,38,33,32,35,34,45,44,47,46,41,40,43,42,53,52,55,54,49,48,51,5..., dimensions={0} | all-to-all | bytes 524288 | tf_op jit(solution)/shard_map/all_to_all | solution.py:278
  57.0 1.0 %backward_x.1 = f32[2,64,512]{2,1,0:T(8,128)} custom-call(f32[512,128]{1,0:T(8,128)S(1)} %bitcast.7, bf16[512,256]{1,0:T(8,128)(2,1)S(1)} %copy-done, bf16[512,256]{1,0:T(8,128)(2,1)S(1)} %copy-done.1), custom_call_target="tpu_custom_call" | custom-call | tf_op jit(solution)/shard_map/backward_x/pallas_call | solution.py:320
Async XLA Ops:
  0.0 0.7 %copy-start.3 = (f32[4,128]{1,0:T(4,128)S(1)}, f32[4,128]{1,0:T(4,128)}, u32[]{:S(2)}) copy-start(f32[4,128]{1,0:T(4,128)} %constant.11.clone.waves_ref) | copy-start | bytes 6148
  0.0 0.7 %copy-start.4 = (f32[128]{0:T(128)S(1)}, f32[128]{0:T(128)}, u32[]{:S(2)}) copy-start(f32[128]{0:T(128)} %param.7) | copy-start | bytes 1540
  2.2 23.4 %copy-start = (bf16[512,256]{1,0:T(8,128)(2,1)S(1)}, bf16[512,256]{1,0:T(8,128)(2,1)}, u32[]{:S(2)}) copy-start(bf16[512,256]{1,0:T(8,128)(2,1)} %constant.8.clone.even_hbm.even_ref) | copy-start | bytes 786436
  2.2 23.4 %copy-start.2 = (bf16[512,256]{1,0:T(8,128)(2,1)S(1)}, bf16[512,256]{1,0:T(8,128)(2,1)}, u32[]{:S(2)}) copy-start(bf16[512,256]{1,0:T(8,128)(2,1)} %constant.10.clone.odd_t_ref) | copy-start | bytes 786436
  26.0 12.3 %copy-start.1 = (bf16[512,256]{1,0:T(8,128)(2,1)S(1)}, bf16[512,256]{1,0:T(8,128)(2,1)}, u32[]{:S(2)}) copy-start(bf16[512,256]{1,0:T(8,128)(2,1)} %constant.9.clone.odd_hbm.odd_ref) | copy-start | bytes 786436

commit v6 on v5

--- a/solution.py
+++ b/solution.py
@@ -83,7 +83,7 @@
 
 def own_place():
     gz, gy = lax.axis_index("gz"), lax.axis_index("gy")
-    return gz >> 3, (((gz & 7) + 8 - Y_IN[0]) & 7) * 8 + ((gy + 8 - G_IN[0]) & 7)
+    return gz >> 3, ((gy + 8 - G_IN[0]) & 7) * 8 + (((gz & 7) + 8 - Y_IN[0]) & 7)
 
 
 def pivots(screening_ref, waves_ref, shift_ref, column_ref, pivot_ref, down_ref, far_ref, close_ref, chunk_ref):
@@ -176,7 +176,7 @@
     keep = lower_half((8, LINES, 128))
 
     def at(g):
-        return blocks[:, G_IN.index(g)]
+        return blocks[G_IN.index(g)]
 
     def gather(parts):
         columns = []
@@ -230,13 +230,13 @@
         for pair in range(2):
             column = values[:, pair * 128 : pair * 128 + 128].reshape(8, 2, LINES, 128)
             a, b = column[:, 0], column[:, 1]
-            out_ref[:, G_OUT.index(base + 2 * pair)] = jnp.where(keep, a, swap_halves(b))
-            out_ref[:, G_OUT.index(base + 2 * pair + 1)] = jnp.where(keep, swap_halves(a), b)
+            out_ref[G_OUT.index(base + 2 * pair)] = jnp.where(keep, a, swap_halves(b))
+            out_ref[G_OUT.index(base + 2 * pair + 1)] = jnp.where(keep, swap_halves(a), b)
 
 
 def backward_x_kernel(rows_ref, even_ref, odd_ref, out_ref):
     blocks = rows_ref[...].reshape(8, 8, LINES, 128)
-    ordered = [blocks[Y_OUT.index(y), G_OUT.index(g)] for y in Y_IN for g in G_IN]
+    ordered = [blocks[G_OUT.index(g), Y_OUT.index(y)] for g in G_IN for y in Y_IN]
     values = jnp.concatenate(ordered, axis=0).T
     even = times_table(values[:, :HALF], even_ref)
     odd = times_table(values[:, HALF:], odd_ref)
@@ -267,7 +267,7 @@
 
 
 def run_peers(along_y, along_g):
-    return [[run * PEERS + y * 8 + g for y in along_y for g in along_g] for run in range(CHUNKS)]
+    return [[run * PEERS + y * 8 + g for g in along_g for y in along_y] for run in range(CHUNKS)]
 
 
 RUNS = [[run * 8 + y for run in RUN_ORDER] for y in range(8)]

time: 58.3 us -> 58.6 us (level)
  no operation moved by 1% of the time
where the time goes in v6:
time: 58.6 us; the launch traced here: 58.3 us
  blocking collectives  54.2 us (92%)
  Pallas kernels  3.35 us (6%)
  local copies, waits for them, and re-layouts  0.7 us (1%)
    all_to_all x2, blocking collectives, exchange_peers(): lax.all_to_all(pieces, ('gz', 'gy'), 0, 0, tiled=True, axis_index_groups=...  41.8 us
    all_to_all x1, blocking collectives, local(): lax.all_to_all(send, 'gz', 0, 0, tiled=True, axis_index_groups=RUNS)  12.4 us
    pallas_call x1, Pallas kernels, local(): call(forward_x_kernel, [VMEM] * 2 + [HBM] * 3, (shape(512, 128), planes,...  1.48 us

profile of v6, /device:TPU:1, one launch (start us, length us, event | category | flops | bytes accessed | tf_op | source)
XLA Modules:
  0.0 58.3 jit_solution(9729075270715117164)
XLA Ops:
  0.0 0.0 copy-start.3
  0.0 0.0 copy-start.4
  0.0 0.7 %copy-done.3 = f32[4,128]{1,0:T(4,128)S(1)} copy-done((f32[4,128]{1,0:T(4,128)S(1)}, f32[4,128]{1,0:T(4,128)}, u32[]{:S(2)}) %copy-start.3) | copy-done | bytes 2072
  0.7 0.0 copy-done.4
  0.7 1.5 %forward_x.1 = (f32[512,128]{1,0:T(8,128)S(1)}, f32[16,8,512]{2,1,0:T(8,128)S(1)}, f32[16,8,512]{2,1,0:T(8,128)S(1)}, f32[8,8,512]{2,1,0:T(8,128)S(1)}, f32[8,512]{1,0:T(8,128)S(1)}, /*index=5*/s32[8,512]{1,0:T(8,128)S(1)}) custom-call(f32[1,128]{1,0:T(1,128)S(1)} %bitcast.9, f32[4,128]{1,0:T(4,128)S(1)} %copy-done.3, f32[2,64,512]{2,1,0:T(8,128)} %source_hbm.1, ...), custom_call_target="tpu_custom_call" | custom-call | tf_op jit(solution)/shard_map/forward_x/pallas_call | solution.py:289
  2.2 0.0 copy-start
  2.2 0.0 copy-start.2
  2.2 23.4 %all_to_all.15 = f32[64,8,128]{2,1,0:T(8,128)S(1)} all-to-all(f32[64,8,128]{2,1,0:T(8,128)S(1)} %bitcast.8), channel_id=1, replica_groups={{39,47,55,63,7,15,23,31,32,40,48,56,0,8,16,24,33,41,49,57,1,9,17,25,34,..., dimensions={0} | all-to-all | bytes 524288 | tf_op jit(solution)/shard_map/all_to_all | solution.py:278
  25.6 0.0 copy-done
  25.7 0.0 copy-done.2
  25.7 0.4 forward_y.1
  26.0 0.0 copy-start.1
  26.0 12.4 %all_to_all.16.arrived_ref = f32[8,8,512]{2,1,0:T(8,128)S(1)} all-to-all(f32[8,8,512]{2,1,0:T(8,128)S(1)} %get-tuple-element.18), channel_id=1, replica_groups={{256,192,320,128,384,64,448,0},{264,200,328,136,392,72,456,8},{272,208,..., dimensions={0} | all-to-all | bytes 262144 | tf_op jit(solution)/shard_map/all_to_all | solution.py:311
  38.5 0.0 copy-done.1
  38.5 0.5 solve.1
  38.9 18.4 %all_to_all.17 = f32[64,8,128]{2,1,0:T(8,128)S(1)} all-to-all(f32[64,8,128]{2,1,0:T(8,128)S(1)} %bitcast.5), channel_id=1, replica_groups={{37,45,53,61,5,13,21,29,36,44,52,60,4,12,20,28,39,47,55,63,7,15,23,31,3..., dimensions={0} | all-to-all | bytes 524288 | tf_op jit(solution)/shard_map/all_to_all | solution.py:278
  57.3 1.0 %backward_x.1 = f32[2,64,512]{2,1,0:T(8,128)} custom-call(f32[512,128]{1,0:T(8,128)S(1)} %bitcast.7, bf16[512,256]{1,0:T(8,128)(2,1)S(1)} %copy-done, bf16[512,256]{1,0:T(8,128)(2,1)S(1)} %copy-done.1), custom_call_target="tpu_custom_call" | custom-call | tf_op jit(solution)/shard_map/backward_x/pallas_call | solution.py:320
Async XLA Ops:
  0.0 0.7 %copy-start.3 = (f32[4,128]{1,0:T(4,128)S(1)}, f32[4,128]{1,0:T(4,128)}, u32[]{:S(2)}) copy-start(f32[4,128]{1,0:T(4,128)} %constant.11.clone.waves_ref) | copy-start | bytes 6148
  0.0 0.7 %copy-start.4 = (f32[128]{0:T(128)S(1)}, f32[128]{0:T(128)}, u32[]{:S(2)}) copy-start(f32[128]{0:T(128)} %param.7) | copy-start | bytes 1540
  2.2 23.5 %copy-start = (bf16[512,256]{1,0:T(8,128)(2,1)S(1)}, bf16[512,256]{1,0:T(8,128)(2,1)}, u32[]{:S(2)}) copy-start(bf16[512,256]{1,0:T(8,128)(2,1)} %constant.8.clone.even_hbm.even_ref) | copy-start | bytes 786436
  2.2 23.5 %copy-start.2 = (bf16[512,256]{1,0:T(8,128)(2,1)S(1)}, bf16[512,256]{1,0:T(8,128)(2,1)}, u32[]{:S(2)}) copy-start(bf16[512,256]{1,0:T(8,128)(2,1)} %constant.10.clone.odd_t_ref) | copy-start | bytes 786436
  26.0 12.4 %copy-start.1 = (bf16[512,256]{1,0:T(8,128)(2,1)S(1)}, bf16[512,256]{1,0:T(8,128)(2,1)}, u32[]{:S(2)}) copy-start(bf16[512,256]{1,0:T(8,128)(2,1)} %constant.9.clone.odd_hbm.odd_ref) | copy-start | bytes 786436

commit v7 on v5

--- a/solution.py
+++ b/solution.py
@@ -197,6 +197,7 @@
     for t in range(RUN):
         plane = modes_ref[row(t, Y_IN)]
         upward = pivot_ref[t] * (plane + upward)
+        modes_ref[row(t, Y_IN)] = upward
         downward = downward + down_ref[t] * plane
     chunk = chunk_ref[...]
     for other in range(CHUNKS):
@@ -212,9 +213,10 @@
         rest = CHUNKS - 1 - other
         above = jnp.where(rest > chunk, arrived_ref[RUN_ORDER.index(rest)] + far_ref[rest] * above, above)
 
-    elimination = below
+    carried = below
     for t in range(RUN):
-        elimination = pivot_ref[t] * (modes_ref[row(t, Y_IN)] + elimination)
+        carried = pivot_ref[t] * carried
+        elimination = modes_ref[row(t, Y_IN)] + carried
         solved_ref[row(t, Y_OUT)] = elimination
     value = (elimination + pivot_ref[RUN - 1] * above) * close_ref[...]
     solved_ref[row(RUN - 1, Y_OUT)] = value

time: 58.3 us -> 58.3 us (level)
  no operation moved by 1% of the time
where the time goes in v7:
time: 58.3 us; the launch traced here: 58 us
  blocking collectives  53.9 us (92%)
  Pallas kernels  3.34 us (6%)
  local copies, waits for them, and re-layouts  0.7 us (1%)
    all_to_all x2, blocking collectives, exchange_peers(): lax.all_to_all(pieces, ('gz', 'gy'), 0, 0, tiled=True, axis_index_groups=...  41.6 us
    all_to_all x1, blocking collectives, local(): lax.all_to_all(send, 'gz', 0, 0, tiled=True, axis_index_groups=RUNS)  12.3 us
    pallas_call x1, Pallas kernels, local(): call(forward_x_kernel, [VMEM] * 2 + [HBM] * 3, (shape(512, 128), planes,...  1.49 us

profile of v7, /device:TPU:1, one launch (start us, length us, event | category | flops | bytes accessed | tf_op | source)
XLA Modules:
  0.0 58.0 jit_solution(17582539503284344894)
XLA Ops:
  0.0 0.0 copy-start.3
  0.0 0.0 copy-start.4
  0.0 0.7 %copy-done.3 = f32[4,128]{1,0:T(4,128)S(1)} copy-done((f32[4,128]{1,0:T(4,128)S(1)}, f32[4,128]{1,0:T(4,128)}, u32[]{:S(2)}) %copy-start.3) | copy-done | bytes 2072
  0.7 0.0 copy-done.4
  0.7 1.5 %forward_x.1 = (f32[512,128]{1,0:T(8,128)S(1)}, f32[16,8,512]{2,1,0:T(8,128)S(1)}, f32[16,8,512]{2,1,0:T(8,128)S(1)}, f32[8,8,512]{2,1,0:T(8,128)S(1)}, f32[8,512]{1,0:T(8,128)S(1)}, /*index=5*/s32[8,512]{1,0:T(8,128)S(1)}) custom-call(f32[1,128]{1,0:T(1,128)S(1)} %bitcast.9, f32[4,128]{1,0:T(4,128)S(1)} %copy-done.3, f32[2,64,512]{2,1,0:T(8,128)} %source_hbm.1, ...), custom_call_target="tpu_custom_call" | custom-call | tf_op jit(solution)/shard_map/forward_x/pallas_call | solution.py:291
  2.2 0.0 copy-start
  2.2 0.0 copy-start.2
  2.2 23.4 %all_to_all.15 = f32[64,8,128]{2,1,0:T(8,128)S(1)} all-to-all(f32[64,8,128]{2,1,0:T(8,128)S(1)} %bitcast.8), channel_id=1, replica_groups={{39,32,33,34,35,36,37,38,47,40,41,42,43,44,45,46,55,48,49,50,51,52,53,5..., dimensions={0} | all-to-all | bytes 524288 | tf_op jit(solution)/shard_map/all_to_all | solution.py:280
  25.6 0.0 copy-done
  25.6 0.0 copy-done.2
  25.6 0.4 forward_y.1
  26.0 0.0 copy-start.1
  26.0 12.3 %all_to_all.16.arrived_ref = f32[8,8,512]{2,1,0:T(8,128)S(1)} all-to-all(f32[8,8,512]{2,1,0:T(8,128)S(1)} %get-tuple-element.18), channel_id=1, replica_groups={{256,192,320,128,384,64,448,0},{264,200,328,136,392,72,456,8},{272,208,..., dimensions={0} | all-to-all | bytes 262144 | tf_op jit(solution)/shard_map/all_to_all | solution.py:313
  38.3 0.0 copy-done.1
  38.3 0.4 solve.1
  38.8 18.2 %all_to_all.17 = f32[64,8,128]{2,1,0:T(8,128)S(1)} all-to-all(f32[64,8,128]{2,1,0:T(8,128)S(1)} %bitcast.5), channel_id=1, replica_groups={{37,36,39,38,33,32,35,34,45,44,47,46,41,40,43,42,53,52,55,54,49,48,51,5..., dimensions={0} | all-to-all | bytes 524288 | tf_op jit(solution)/shard_map/all_to_all | solution.py:280
  57.0 1.0 %backward_x.1 = f32[2,64,512]{2,1,0:T(8,128)} custom-call(f32[512,128]{1,0:T(8,128)S(1)} %bitcast.7, bf16[512,256]{1,0:T(8,128)(2,1)S(1)} %copy-done, bf16[512,256]{1,0:T(8,128)(2,1)S(1)} %copy-done.1), custom_call_target="tpu_custom_call" | custom-call | tf_op jit(solution)/shard_map/backward_x/pallas_call | solution.py:322
Async XLA Ops:
  0.0 0.7 %copy-start.3 = (f32[4,128]{1,0:T(4,128)S(1)}, f32[4,128]{1,0:T(4,128)}, u32[]{:S(2)}) copy-start(f32[4,128]{1,0:T(4,128)} %constant.11.clone.waves_ref) | copy-start | bytes 6148
  0.0 0.7 %copy-start.4 = (f32[128]{0:T(128)S(1)}, f32[128]{0:T(128)}, u32[]{:S(2)}) copy-start(f32[128]{0:T(128)} %param.7) | copy-start | bytes 1540
  2.2 23.4 %copy-start = (bf16[512,256]{1,0:T(8,128)(2,1)S(1)}, bf16[512,256]{1,0:T(8,128)(2,1)}, u32[]{:S(2)}) copy-start(bf16[512,256]{1,0:T(8,128)(2,1)} %constant.8.clone.even_hbm.even_ref) | copy-start | bytes 786436
  2.2 23.4 %copy-start.2 = (bf16[512,256]{1,0:T(8,128)(2,1)S(1)}, bf16[512,256]{1,0:T(8,128)(2,1)}, u32[]{:S(2)}) copy-start(bf16[512,256]{1,0:T(8,128)(2,1)} %constant.10.clone.odd_t_ref) | copy-start | bytes 786436
  26.0 12.3 %copy-start.1 = (bf16[512,256]{1,0:T(8,128)(2,1)S(1)}, bf16[512,256]{1,0:T(8,128)(2,1)}, u32[]{:S(2)}) copy-start(bf16[512,256]{1,0:T(8,128)(2,1)} %constant.9.clone.odd_hbm.odd_ref) | copy-start | bytes 786436

commit v8 on v7

--- a/solution.py
+++ b/solution.py
@@ -19,7 +19,7 @@
 PEERS = 64
 RUN_ORDER = (4, 3, 5, 2, 6, 1, 7, 0)
 Y_IN = (4, 5, 6, 7, 0, 1, 2, 3)
-G_IN = (7, 0, 1, 2, 3, 4, 5, 6)
+G_IN = (5, 6, 7, 0, 1, 2, 3, 4)
 Y_OUT = (4, 5, 6, 7, 0, 1, 2, 3)
 G_OUT = (5, 4, 7, 6, 1, 0, 3, 2)
 

time: 58.3 us -> 58.1 us (level)
  no operation moved by 1% of the time
where the time goes in v8:
time: 58.1 us; the launch traced here: 57.8 us
  blocking collectives  53.7 us (92%)
  Pallas kernels  3.34 us (6%)
  local copies, waits for them, and re-layouts  0.7 us (1%)
    all_to_all x2, blocking collectives, exchange_peers(): lax.all_to_all(pieces, ('gz', 'gy'), 0, 0, tiled=True, axis_index_groups=...  41.2 us
    all_to_all x1, blocking collectives, local(): lax.all_to_all(send, 'gz', 0, 0, tiled=True, axis_index_groups=RUNS)  12.6 us
    pallas_call x1, Pallas kernels, local(): call(forward_x_kernel, [VMEM] * 2 + [HBM] * 3, (shape(512, 128), planes,...  1.49 us

profile of v8, /device:TPU:1, one launch (start us, length us, event | category | flops | bytes accessed | tf_op | source)
XLA Modules:
  0.0 57.8 jit_solution(1025204123686108124)
XLA Ops:
  0.0 0.0 copy-start.3
  0.0 0.0 copy-start.4
  0.0 0.7 %copy-done.3 = f32[4,128]{1,0:T(4,128)S(1)} copy-done((f32[4,128]{1,0:T(4,128)S(1)}, f32[4,128]{1,0:T(4,128)}, u32[]{:S(2)}) %copy-start.3) | copy-done | bytes 2072
  0.7 0.0 copy-done.4
  0.7 1.5 %forward_x.1 = (f32[512,128]{1,0:T(8,128)S(1)}, f32[16,8,512]{2,1,0:T(8,128)S(1)}, f32[16,8,512]{2,1,0:T(8,128)S(1)}, f32[8,8,512]{2,1,0:T(8,128)S(1)}, f32[8,512]{1,0:T(8,128)S(1)}, /*index=5*/s32[8,512]{1,0:T(8,128)S(1)}) custom-call(f32[1,128]{1,0:T(1,128)S(1)} %bitcast.9, f32[4,128]{1,0:T(4,128)S(1)} %copy-done.3, f32[2,64,512]{2,1,0:T(8,128)} %source_hbm.1, ...), custom_call_target="tpu_custom_call" | custom-call | tf_op jit(solution)/shard_map/forward_x/pallas_call | solution.py:291
  2.2 0.0 copy-start
  2.2 0.0 copy-start.2
  2.2 23.3 %all_to_all.15 = f32[64,8,128]{2,1,0:T(8,128)S(1)} all-to-all(f32[64,8,128]{2,1,0:T(8,128)S(1)} %bitcast.8), channel_id=1, replica_groups={{37,38,39,32,33,34,35,36,45,46,47,40,41,42,43,44,53,54,55,48,49,50,51,5..., dimensions={0} | all-to-all | bytes 524288 | tf_op jit(solution)/shard_map/all_to_all | solution.py:280
  25.5 0.0 copy-done
  25.5 0.0 copy-done.2
  25.5 0.4 forward_y.1
  25.9 0.0 copy-start.1
  25.9 12.6 %all_to_all.16.arrived_ref = f32[8,8,512]{2,1,0:T(8,128)S(1)} all-to-all(f32[8,8,512]{2,1,0:T(8,128)S(1)} %get-tuple-element.18), channel_id=1, replica_groups={{256,192,320,128,384,64,448,0},{264,200,328,136,392,72,456,8},{272,208,..., dimensions={0} | all-to-all | bytes 262144 | tf_op jit(solution)/shard_map/all_to_all | solution.py:313
  38.5 0.0 copy-done.1
  38.5 0.4 solve.1
  39.0 17.8 %all_to_all.17 = f32[64,8,128]{2,1,0:T(8,128)S(1)} all-to-all(f32[64,8,128]{2,1,0:T(8,128)S(1)} %bitcast.5), channel_id=1, replica_groups={{37,36,39,38,33,32,35,34,45,44,47,46,41,40,43,42,53,52,55,54,49,48,51,5..., dimensions={0} | all-to-all | bytes 524288 | tf_op jit(solution)/shard_map/all_to_all | solution.py:280
  56.8 1.0 %backward_x.1 = f32[2,64,512]{2,1,0:T(8,128)} custom-call(f32[512,128]{1,0:T(8,128)S(1)} %bitcast.7, bf16[512,256]{1,0:T(8,128)(2,1)S(1)} %copy-done, bf16[512,256]{1,0:T(8,128)(2,1)S(1)} %copy-done.1), custom_call_target="tpu_custom_call" | custom-call | tf_op jit(solution)/shard_map/backward_x/pallas_call | solution.py:322
Async XLA Ops:
  0.0 0.7 %copy-start.3 = (f32[4,128]{1,0:T(4,128)S(1)}, f32[4,128]{1,0:T(4,128)}, u32[]{:S(2)}) copy-start(f32[4,128]{1,0:T(4,128)} %constant.11.clone.waves_ref) | copy-start | bytes 6148
  0.0 0.7 %copy-start.4 = (f32[128]{0:T(128)S(1)}, f32[128]{0:T(128)}, u32[]{:S(2)}) copy-start(f32[128]{0:T(128)} %param.7) | copy-start | bytes 1540
  2.2 23.3 %copy-start = (bf16[512,256]{1,0:T(8,128)(2,1)S(1)}, bf16[512,256]{1,0:T(8,128)(2,1)}, u32[]{:S(2)}) copy-start(bf16[512,256]{1,0:T(8,128)(2,1)} %constant.8.clone.even_hbm.even_ref) | copy-start | bytes 786436
  2.2 23.3 %copy-start.2 = (bf16[512,256]{1,0:T(8,128)(2,1)S(1)}, bf16[512,256]{1,0:T(8,128)(2,1)}, u32[]{:S(2)}) copy-start(bf16[512,256]{1,0:T(8,128)(2,1)} %constant.10.clone.odd_t_ref) | copy-start | bytes 786436
  25.9 12.6 %copy-start.1 = (bf16[512,256]{1,0:T(8,128)(2,1)S(1)}, bf16[512,256]{1,0:T(8,128)(2,1)}, u32[]{:S(2)}) copy-start(bf16[512,256]{1,0:T(8,128)(2,1)} %constant.9.clone.odd_hbm.odd_ref) | copy-start | bytes 786436
